TPU v7x, 128 devices: a whole 4x4x4 slice. The times are simulated.
128 devices in a mesh: dp: 64 (over x, y_lo, z, core), tensor: 2 (over y_hi).
Axes of the slice: x: 4, y: 4 (y_hi: 2, y_lo: 2; y = y_hi * 2 + y_lo), z: 4, core: 2. Of those that a mesh axis runs over, the one named last changes fastest.
Arguments:
- image_cache: bfloat16 [8192, 1280], P('dp'), may hold values from -0.3 to 0.3
- text_cache: bfloat16 [8192, 1280], P('dp'), may hold values from -0.3 to 0.3
- labels: int32 [8192], P('dp'), may hold values from 0 to 8191, each once
- layer_input: bfloat16 [8192, 1664], P('dp'), may hold values from -16 to 16
- ln1_gain: float32 [1664], replicated, may hold values from 0.25 to 1.75
- ln2_gain: float32 [1664], replicated, may hold values from 0.25 to 1.75
- w_up: bfloat16 [1664, 4096], P(None, 'tensor'), may hold values from -0.15625 to 0.15625
- w_down: bfloat16 [1664, 4096], P(None, 'tensor'), may hold values from -0.09375 to 0.09375
- proj: bfloat16 [1664, 1280], replicated, may hold values from -0.15625 to 0.15625
Outputs:
- text_grad: bfloat16 [8192, 1280], P('dp')
- input_grad: bfloat16 [8192, 1664], P('dp')
- up_grad: float32 [1664, 4096], P('dp', 'tensor')
- proj_grad: float32 [1664, 1280], P('dp', 'tensor')
All inputs are finite; a program needn't handle non-finite values.
Results may differ from a plain program's by a relative error of at most 0.013.
Values may be sent and summed in bfloat16 or wider, within the bound.
A program may use at most 128 MiB of HBM per device.

v0:
```python
import jax
import jax.numpy as jnp
from jax import lax
from jax.sharding import PartitionSpec as P

logit_scale = 100.0


def combined_all(part, axis, combine):
    gathered = jax.tree.map(lambda a: lax.all_gather(a, axis), part)

    def take(source):
        return jax.tree.map(lambda a: lax.dynamic_index_in_dim(a, source, 0, False), gathered)

    return lax.fori_loop(
        1, lax.axis_size(axis), lambda source, state: combine(state, take(source)), take(0)
    )


def unit_rows(values):
    floats = values.astype(jnp.float32)
    inverse = lax.rsqrt(jnp.sum(floats * floats, axis=1, keepdims=True) + 1e-06)
    return (floats * inverse, inverse)


def unit_back(normed, inverse, grad):
    return inverse * (grad - normed * jnp.sum(grad * normed, axis=1, keepdims=True))


def layer_norm(values):
    center = values - jnp.mean(values, axis=1, keepdims=True)
    scale_inv = lax.rsqrt(jnp.mean(center * center, axis=1, keepdims=True) + 1e-05)
    return (center * scale_inv, scale_inv)


def norm_back(grad, normed, scale_inv):
    return scale_inv * (
        grad
        - jnp.mean(grad, axis=1, keepdims=True)
        - normed * jnp.mean(grad * normed, axis=1, keepdims=True)
    )


def gelu_slope(values):
    return (
        0.5 * (1.0 + lax.erf(values * 0.7071067811865476))
        + values * jnp.exp(-0.5 * values * values) * 0.3989422804014327
    )


def contract_last(left, right):
    return lax.dot_general(
        left, right, (((1,), (1,)), ((), ())), preferred_element_type=jnp.float32
    )


def contract_first(left, right):
    return lax.dot_general(
        left, right, (((0,), (0,)), ((), ())), preferred_element_type=jnp.float32
    )


def combine_stats(first, second):
    merged = []
    for place in range(0, len(first), 2):
        peak = jnp.maximum(first[place], second[place])
        total = first[place + 1] * jnp.exp(first[place] - peak) + second[place + 1] * jnp.exp(
            second[place] - peak
        )
        merged.append(peak)
        merged.append(total)
    return tuple(merged)


def peak_total(logits, axis):
    peak = jnp.max(logits, axis=axis)
    total = jnp.sum(jnp.exp(logits - jnp.expand_dims(peak, axis)), axis=axis)
    return (peak, total)


def local(image_cache, text_cache, labels, layer_input, ln1_gain, ln2_gain, w_up, w_down, proj):
    rows = image_cache.shape[0]
    pair_count = lax.axis_size("tensor")
    side = lax.axis_index("tensor")
    group = lax.axis_index("dp")
    half = rows // pair_count
    embed_half = proj.shape[1] // pair_count
    offset = side * half
    img_norm, img_inv = unit_rows(image_cache)
    txt_norm, txt_inv = unit_rows(text_cache)
    img_unit = img_norm.astype(jnp.bfloat16)
    txt_unit = txt_norm.astype(jnp.bfloat16)
    far_txt, far_img = (
        lax.all_gather(
            lax.dynamic_slice_in_dim(txt_unit, offset, half, 0), "dp", axis=0, tiled=True
        ),
        lax.all_gather(
            lax.dynamic_slice_in_dim(img_unit, offset, half, 0), "dp", axis=0, tiled=True
        ),
    )
    far_labels = lax.all_gather(
        lax.dynamic_slice_in_dim(labels, offset, half, 0), "dp", axis=0, tiled=True
    )
    positions = jnp.arange(far_txt.shape[0], dtype=jnp.int32)
    far_index = positions // half * rows + offset + positions % half
    own_index = group * rows + jnp.arange(rows, dtype=jnp.int32)
    inputs = layer_input.astype(jnp.float32)
    normed_in, inv_in = layer_norm(inputs)
    mlp_in = (normed_in * ln1_gain).astype(jnp.bfloat16)
    pre = jnp.dot(mlp_in, w_up, preferred_element_type=jnp.float32)
    act = jax.nn.gelu(pre, approximate=False).astype(jnp.bfloat16)
    resid = inputs + lax.psum(contract_last(act, w_down), "tensor")
    normed_out, inv_out = layer_norm(resid)
    pooled = (normed_out * ln2_gain).astype(jnp.bfloat16)
    logit_a = logit_scale * contract_last(img_unit, far_txt)
    logit_b = logit_scale * contract_last(txt_unit, far_img)
    row_peak, row_total = peak_total(logit_a, 1)
    col_peak, col_total = peak_total(logit_b, 1)
    merged = combined_all((row_peak, row_total, col_peak, col_total), "tensor", combine_stats)
    row_lse = merged[0] + jnp.log(merged[1])
    col_lse = merged[2] + jnp.log(merged[3])
    far_col_lse, far_row_lse = (
        lax.all_gather(
            lax.dynamic_slice_in_dim(col_lse, offset, half, 0), "dp", axis=0, tiled=True
        ),
        lax.all_gather(
            lax.dynamic_slice_in_dim(row_lse, offset, half, 0), "dp", axis=0, tiled=True
        ),
    )
    match_a = (labels[:, None] == far_index[None, :]).astype(jnp.float32)
    grad_a = (
        0.5 * (jnp.exp(logit_a - row_lse[:, None]) + jnp.exp(logit_a - far_col_lse[None, :]))
        - match_a
    ).astype(jnp.bfloat16)
    match_b = (own_index[:, None] == far_labels[None, :]).astype(jnp.float32)
    grad_b = (
        0.5 * (jnp.exp(logit_b - far_row_lse[None, :]) + jnp.exp(logit_b - col_lse[:, None]))
        - match_b
    ).astype(jnp.bfloat16)
    part_img = logit_scale * jnp.dot(grad_a, far_txt, preferred_element_type=jnp.float32)
    part_txt = logit_scale * jnp.dot(grad_b, far_img, preferred_element_type=jnp.float32)
    img_unit_grad, txt_unit_grad = lax.psum((part_img, part_txt), "tensor")
    image_grad = unit_back(img_norm, img_inv, img_unit_grad)
    text_grad = unit_back(txt_norm, txt_inv, txt_unit_grad).astype(jnp.bfloat16)
    cotangent = image_grad.astype(jnp.bfloat16)
    cot_half = lax.dynamic_slice_in_dim(cotangent, side * embed_half, embed_half, 1)
    pooled_grad = contract_last(cotangent, proj)
    resid_grad = norm_back(pooled_grad * ln2_gain, normed_out, inv_out)
    resid_cot = resid_grad.astype(jnp.bfloat16)
    pre_grad = (
        jnp.dot(resid_cot, w_down, preferred_element_type=jnp.float32) * gelu_slope(pre)
    ).astype(jnp.bfloat16)
    mlp_in_grad = lax.psum(contract_last(pre_grad, w_up).astype(jnp.bfloat16), "tensor").astype(
        jnp.float32
    )
    input_grad = (resid_grad + norm_back(mlp_in_grad * ln1_gain, normed_in, inv_in)).astype(
        jnp.bfloat16
    )
    summed = lax.psum_scatter(
        jnp.concatenate(
            [contract_first(mlp_in, pre_grad), contract_first(pooled, cot_half)], axis=1
        ),
        "dp",
        scatter_dimension=0,
        tiled=True,
    )
    hidden = pre_grad.shape[1]
    up_grad = summed[:, :hidden]
    proj_grad = summed[:, hidden:]
    return (text_grad, input_grad, up_grad, proj_grad)


def solution(mesh):
    in_specs = (
        P("dp", None),
        P("dp", None),
        P("dp"),
        P("dp", None),
        P(),
        P(),
        P(None, "tensor"),
        P(None, "tensor"),
        P(),
    )
    out_specs = (P("dp", None), P("dp", None), P("dp", "tensor"), P("dp", "tensor"))
    return jax.shard_map(local, mesh=mesh, in_specs=in_specs, out_specs=out_specs, check_vma=False)
```

profile of v0, /device:TPU:1, one launch (start us, length us, event | category | flops | bytes accessed | tf_op | source)
XLA Modules:
  0.0 1373.5 jit_solution(17604469466316987736)
XLA Ops:
  7.2 0.0 copy-start.13
  7.2 0.0 all-gather.11.cloned.1.call-start
  7.3 1.2 fusion.53
  8.4 1.1 fusion.40
  9.5 0.7 constant_dynamic-slice_fusion.1
  10.2 0.0 all-gather.11.cloned.1.call-update
  10.3 0.0 all-gather.13.cloned.1.call-start
  10.3 1.1 fusion.48
  11.4 1.1 fusion.43
  12.5 0.7 constant_dynamic-slice_fusion
  13.2 0.0 all-gather.13.cloned.1.call-update
  13.2 0.0 all-reduce.14.cloned.1.call-start
  13.3 0.6 fusion.149
  14.6 0.2 dynamic-slice_dynamic-update-slice_fusion.1
  14.8 277.5 %all-reduce.1 = s32[4096]{0:T(1024)S(1)} all-reduce(s32[4096]{0:T(1024)S(1)} %dynamic-slice_dynamic-update-slice_fusion.1), channel_id=1, replica_groups=mesh['dp'=64,'tensor'=2] {'dp'}, use_global_device_ids=true, to_apply=%add.1 | all-reduce | flops 4096 | bytes 32768
  292.3 0.1 convert_reduce_fusion
  292.4 0.3 fusion.36
  292.7 0.0 slice-start.3
  292.7 4.2 fusion.145
  297.0 1.1 copy-done.7
  298.0 5.0 fusion.54
  303.1 7.5 fusion.150
  310.6 1.3 copy-done.2
  312.0 0.4 exponential_reduce_fusion
  312.4 4.6 all-gather.7
  317.0 4.6 all-gather.6
  321.5 7.6 fusion.151
  329.1 1.3 copy-done.4
  330.4 0.4 exponential_reduce_fusion.1
  330.9 4.7 all-gather.5
  335.6 4.6 all-gather.4
  340.2 0.2 dynamic-slice_dynamic-update-slice_fusion.2
  340.4 0.2 dynamic-slice_dynamic-update-slice_fusion
  340.5 279.5 %all-reduce.4 = (f32[4096]{0:T(1024)S(1)}, f32[4096]{0:T(1024)S(1)}) all-reduce(f32[4096]{0:T(1024)S(1)} %dynamic-slice_dynamic-update-slice_fusion.2, f32[4096]{0:T(1024)S(1)} %dynamic-slice_dynamic-update-slice_fusion), channel_id=1, replica_groups=mesh['dp'=64,'tensor'=2] {'dp'}, use_global_device_ids=true, to_apply=%add | all-reduce | flops 8192 | bytes 65536
  620.0 7.7 convolution_multiply_fusion.2
  627.7 2.9 convolution_multiply_fusion.3
  630.6 0.0 all-reduce.14.cloned.1.call-update
  630.7 0.0 all-reduce.10.cloned.1.call-start
  630.7 75.0 %all-reduce.14.cloned.1.call-done = (f32[128,1280]{1,0:T(8,128)}, f32[128,1280]{1,0:T(8,128)}, f32[128,1664]{1,0:T(8,128)}) async-done(((f32[128,1280]{1,0:T(8,128)}, f32[128,1280]{1,0:T(8,128)}, f32[128,1664]{1,0:T(8,128)}), (f32[128,1280]{1,0:T(8,128)}, f32[128,1280]{1,0:T(8,128)}, f32[128,1664]{1,0:T(8,128)})) %all-reduce.14.cloned.1.call-update) | async-done | bytes 2162704 | tf_op jit(solution)/shard_map/psum | solution.py:142
  705.8 1.4 fusion.147
  707.2 1.5 multiply_reduce_fusion.1
  708.7 0.2 fusion.49
  708.9 0.3 fusion.52
  709.2 0.0 slice-start
  709.2 3.9 fusion.148
  713.2 0.0 slice-start.1
  713.2 4.8 fusion
  718.0 3.1 convolution_convert_fusion
  721.1 6.9 fusion.143
  728.0 0.0 all-reduce.10.cloned.1.call-update
  728.1 0.3 all-reduce.12.cloned.1.call-start
  728.3 0.8 fusion.86
  729.2 11.5 pad_maximum_fusion
  740.7 0.0 all-reduce.12.cloned.1.call-update
  741.4 0.2 copy-done.6
  741.7 0.2 copy-done.9
  741.9 0.2 fusion.44
  742.1 1.0 fusion.47
  743.1 19.1 %all-reduce.10.cloned.1.call-done = bf16[128,1664]{1,0:T(8,128)(2,1)} async-done(((bf16[128,1664]{1,0:T(8,128)(2,1)}), bf16[128,1664]{1,0:T(8,128)(2,1)}) %all-reduce.10.cloned.1.call-update) | async-done | bytes 426000 | tf_op jit(solution)/shard_map/psum | solution.py:153
  762.2 1.3 fusion.37
  763.5 2.4 fusion.35
  765.9 597.7 %all-reduce.12.cloned.1.call-done = f32[1664,2688]{1,0:T(8,128)} async-done(((f32[1664,2688]{1,0:T(8,128)}), f32[1664,2688]{1,0:T(8,128)}) %all-reduce.12.cloned.1.call-update) | async-done | bytes 17891344
  1363.7 1.7 constant_dynamic-slice_fusion.2
  1365.4 1.6 dynamic-slice.6
  (56 shorter events, 0.2 us)
Async XLA Ops:
  7.2 6.1 copy-start.13
  7.2 7.4 copy-start.14
  7.2 285.1 %copy-start = (bf16[128,1664]{1,0:T(8,128)(2,1)S(1)}, bf16[128,1664]{1,0:T(8,128)(2,1)}, u32[]{:S(2)}) copy-start(bf16[128,1664]{1,0:T(8,128)(2,1)} %param.12) | copy-start | bytes 1277956
  7.2 285.5 %copy-start.11 = (f32[1664]{0:T(1024)S(1)}, f32[1664]{0:T(1024)}, u32[]{:S(2)}) copy-start(f32[1664]{0:T(1024)} %param.13) | copy-start | bytes 19972
  7.2 295.9 %all-gather.11.cloned.1.call-start = ((), (), s32[]{:S(2)}) async-start(), calls=%async_computation | async-start | bytes 10649600 | tf_op jit(solution)/shard_map/all_gather | solution.py:97
  10.3 311.3 %all-gather.13.cloned.1.call-start = ((), (), s32[]{:S(2)}) async-start(), calls=%async_computation.1 | async-start | bytes 10649600 | tf_op jit(solution)/shard_map/all_gather | solution.py:94
  13.2 692.5 %all-reduce.14.cloned.1.call-start = ((), (), s32[]{:S(2)}) async-start(), calls=%async_computation.4 | async-start | bytes 4325376 | tf_op jit(solution)/shard_map/psum | solution.py:142
  292.4 5.6 slice-start.2
  292.7 5.3 slice-start.3
  297.0 1.1 copy-start.7
  310.6 1.3 copy-start.2
  329.1 1.4 copy-start.4
  330.4 297.3 %slice-start.4 = ((s8[10485760]{0:T(1024)(128)(4,1)}), s8[2097152]{0:T(1024)(128)(4,1)S(1)}, s32[]{:S(2)}) async-start(s8[10485760]{0:T(1024)(128)(4,1)} %bitcast.72), calls=%async_computation.9 | async-start | bytes 4194304
  620.0 7.7 slice-start.5
  620.0 7.7 slice-start.6
  620.0 7.7 copy-start.3
  630.6 78.0 %copy-start.5 = (bf16[128,1280]{1,0:T(8,128)(2,1)S(1)}, bf16[128,1280]{1,0:T(8,128)(2,1)}, u32[]{:S(2)}) copy-start(bf16[128,1280]{1,0:T(8,128)(2,1)} %param.9) | copy-start | bytes 983044
  630.7 131.5 %all-reduce.10.cloned.1.call-start = ((), (), s32[]{:S(2)}) async-start(), calls=%async_computation.2 | async-start | bytes 851968 | tf_op jit(solution)/shard_map/psum | solution.py:153
  705.8 2.9 copy-start.10
  707.2 2.0 copy-start.1
  707.2 2.0 copy-start.12
  709.2 3.9 copy-start.8
  709.2 8.8 slice-start
  713.2 4.8 slice-start.1
  728.1 635.6 %all-reduce.12.cloned.1.call-start = ((), (), s32[]{:S(2)}) async-start(), calls=%async_computation.3 | async-start | bytes 35782656
  740.7 1.0 copy-start.6
  740.7 1.2 copy-start.9
Sparse Core Ops, SparseCore 0:
  10.4 118.7 all-gather.10
  131.4 114.1 all-gather.12
  630.8 74.9 all-reduce.13
  728.2 33.9 all-reduce.9
  764.7 598.9 all-reduce.11
where the time goes:
time: 1380 us; the launch traced here: 1370 us
  waiting for transfers between devices  692 us (50%)
  blocking collectives  575 us (42%)
  matrix products  54.5 us (4%)
  other arithmetic  25.7 us (2%)
  between operations  15.5 us (1%)
    unnamed x6, waiting for transfers between devices  598 us
    unnamed x2, blocking collectives  557 us
    psum x1, waiting for transfers between devices, local(): img_unit_grad, txt_unit_grad = lax.psum((part_img, part_txt), 'tensor')  75 us
  transfers between devices with their start and end apart: 5, of which 3 were waited for; matrix products, arithmetic and copies ran while one was open for 3% of the time, Pallas kernels for 0%

commit v1 on v0

v1 whole, which is shorter than its diff:
```python
import jax
import jax.numpy as jnp
from jax import lax
from jax.experimental import pallas as pl
from jax.experimental.pallas import tpu as pltpu
from jax.sharding import PartitionSpec as P

logit_scale = 100.0
MESH = pl.DeviceIdType.MESH
NX, NYL, NZ, NC = 4, 2, 4, 2
bf16 = jnp.bfloat16
f32 = jnp.float32


def dp_of(x, yl, z, c):
    return ((x * NYL + yl) * NZ + z) * NC + c


def coords():
    d = lax.axis_index("dp")
    c = d % NC
    z = (d // NC) % NZ
    yl = (d // (NC * NZ)) % NYL
    x = d // (NC * NZ * NYL)
    return x, yl, z, c, lax.axis_index("tensor")


def barrier(peers):
    sem = pltpu.get_barrier_semaphore()
    for peer in peers:
        pl.semaphore_signal(sem, inc=1, device_id=peer, device_id_type=MESH)
    pl.semaphore_wait(sem, len(peers))


class Comm:
    def __init__(self, send_sem, recv_sem):
        self.send_sem, self.recv_sem, self.n = send_sem, recv_sem, 0

    def send(self, src, dst, dev):
        i = self.n
        self.n += 1
        copy = pltpu.make_async_remote_copy(
            src_ref=src,
            dst_ref=dst,
            send_sem=self.send_sem.at[i],
            recv_sem=self.recv_sem.at[i],
            device_id=dev,
            device_id_type=MESH,
        )
        copy.start()
        return copy


def comm_call(kernel, out_shapes, in_spaces, out_spaces, scratch, n_sems, n_local, cid, *args):
    return pl.pallas_call(
        kernel,
        out_shape=out_shapes,
        in_specs=[pl.BlockSpec(memory_space=s) for s in in_spaces],
        out_specs=[pl.BlockSpec(memory_space=s) for s in out_spaces],
        scratch_shapes=list(scratch)
        + [
            pltpu.SemaphoreType.DMA((n_sems,)),
            pltpu.SemaphoreType.DMA((n_sems,)),
            pltpu.SemaphoreType.DMA((n_local,)),
        ],
        compiler_params=pltpu.CompilerParams(
            collective_id=cid, has_side_effects=True, vmem_limit_bytes=40 * 1024 * 1024
        ),
    )(*args)


def z_peers(x, yl, z, c, t):
    return [(dp_of(x, yl, (z + k) % NZ, c), t) for k in range(1, NZ)]


def xy_offsets():
    return [(kx, ky) for kx in range(NX) for ky in range(NYL) if (kx, ky) != (0, 0)]


def xy_peers(x, yl, z, c, t):
    return [(dp_of((x + kx) % NX, (yl + ky) % NYL, z, c), t) for kx, ky in xy_offsets()]


def gather_kernel(img, txt, lab, mlp, res, img_all, txt_all, lab_all, mlp_all, res_in, ss, rs, ls):
    x, yl, z, c, t = coords()
    sib = (dp_of(x, yl, z, 1 - c), t)
    mate = (lax.axis_index("dp"), 1 - t)
    zp, xp = z_peers(x, yl, z, c, t), xy_peers(x, yl, z, c, t)
    barrier([sib, mate] + zp + xp)
    comm = Comm(ss, rs)
    own = [
        pltpu.make_async_copy(img, img_all.at[z], ls.at[0]),
        pltpu.make_async_copy(txt, txt_all.at[c, x * NYL + yl], ls.at[1]),
        pltpu.make_async_copy(lab, lab_all.at[z], ls.at[2]),
        pltpu.make_async_copy(mlp, mlp_all.at[z * NC + c], ls.at[3]),
    ]
    for copy in own:
        copy.start()
    img_sends = [comm.send(img, img_all.at[z], p) for p in zp]
    txt_sends = [comm.send(txt, txt_all.at[c, x * NYL + yl], p) for p in xp]
    rest = [comm.send(lab, lab_all.at[z], p) for p in zp]
    rest.append(comm.send(txt, txt_all.at[c, x * NYL + yl], sib))
    rest.append(comm.send(res, res_in, mate))
    mlp_sends = [comm.send(mlp, mlp_all.at[z * NC + c], p) for p in zp]
    rest.append(comm.send(mlp, mlp_all.at[z * NC + c], sib))
    for (kx, ky), copy in zip(xy_offsets(), txt_sends):
        copy.wait_recv()
        slot = ((x + NX - kx) % NX) * NYL + (yl + ky) % NYL
        rest.append(comm.send(txt_all.at[c, slot], txt_all.at[c, slot], sib))
    for k, copy in zip(range(1, NZ), mlp_sends):
        copy.wait_recv()
        slot = ((z + NZ - k) % NZ) * NC + c
        rest.append(comm.send(mlp_all.at[slot], mlp_all.at[slot], sib))
    for copy in img_sends + rest:
        copy.wait()
    for copy in txt_sends + mlp_sends:
        copy.wait_send()
    for copy in own:
        copy.wait()


def stats_kernel(rows, cols, rows_all, cols_all, ss, rs, ls):
    x, yl, z, c, t = coords()
    row_peers = [
        (dp_of(x, yl, (z + k) % NZ, c), (t + j) % 2) for k in range(NZ) for j in range(2) if k or j
    ]
    col_peers = [
        (dp_of((x + kx) % NX, (yl + ky) % NYL, z, (c + kc) % NC), t)
        for kx in range(NX)
        for ky in range(NYL)
        for kc in range(NC)
        if kx or ky or kc
    ]
    barrier(row_peers + col_peers)
    comm = Comm(ss, rs)
    sends = [comm.send(rows, rows_all.at[z * 2 + t], p) for p in row_peers]
    mine = (x * NYL + yl) * NC + c
    sends += [comm.send(cols, cols_all.at[mine], p) for p in col_peers]
    rows_all[z * 2 + t] = rows[...]
    cols_all[mine] = cols[...]
    for copy in sends:
        copy.wait()


def reduce_kernel(
    pimg, ptxt, pooled, img_two, txt_sum, pooled_all, img_in, sib_in, txt_out, txt_in, ss, rs, ls
):
    x, yl, z, c, t = coords()
    sib = (dp_of(x, yl, z, 1 - c), t)
    mate = (lax.axis_index("dp"), 1 - t)
    zp, xp = z_peers(x, yl, z, c, t), xy_peers(x, yl, z, c, t)
    barrier([sib, mate] + zp + xp)
    comm = Comm(ss, rs)
    first = comm.send(ptxt.at[1 - c], sib_in, sib)
    img_sends = [
        comm.send(pimg.at[(z + k) % NZ], img_in.at[k - 1], p) for k, p in zip(range(1, NZ), zp)
    ]
    own = pltpu.make_async_copy(pooled, pooled_all.at[z * NC + c], ls.at[0])
    own.start()
    first.wait()
    txt_sends = []
    for i, ((kx, ky), p) in enumerate(zip(xy_offsets(), xp)):
        slot = ((x + kx) % NX) * NYL + (yl + ky) % NYL
        txt_out[i] = (ptxt[c, slot].astype(f32) + sib_in[slot].astype(f32)).astype(bf16)
        txt_sends.append(comm.send(txt_out.at[i], txt_in.at[i], p))
    pooled_sends = [comm.send(pooled, pooled_all.at[z * NC + c], p) for p in zp]
    rest = [comm.send(pooled, pooled_all.at[z * NC + c], sib)]
    for copy in img_sends:
        copy.wait()
    total = pimg[z].astype(f32)
    for k in range(NZ - 1):
        total = total + img_in[k].astype(f32)
    img_two[0] = total.astype(bf16)
    rest.append(comm.send(img_two.at[0], img_two.at[1], mate))
    mine = x * NYL + yl
    total = ptxt[c, mine].astype(f32) + sib_in[mine].astype(f32)
    for i, copy in enumerate(txt_sends):
        copy.wait()
        total = total + txt_in[i].astype(f32)
    txt_sum[...] = total
    for k, copy in zip(range(1, NZ), pooled_sends):
        copy.wait_recv()
        slot = ((z + NZ - k) % NZ) * NC + c
        rest.append(comm.send(pooled_all.at[slot], pooled_all.at[slot], sib))
    for copy in pooled_sends:
        copy.wait_send()
    for copy in rest:
        copy.wait()
    own.wait()


def zc_offsets():
    return [(kz, kc) for kz in range(NZ) for kc in range(NC) if (kz, kc) != (0, 0)]


def zc_peers(x, yl, z, c, t):
    return [(dp_of(x, yl, (z + kz) % NZ, (c + kc) % NC), t) for kz, kc in zc_offsets()]


def swap_kernel(pre, cot, mg, txt, pre_all, cot_all, mg_in, txt_in, ss, rs, ls):
    x, yl, z, c, t = coords()
    mate = (lax.axis_index("dp"), 1 - t)
    zc = zc_peers(x, yl, z, c, t)
    barrier([mate] + zc)
    comm = Comm(ss, rs)
    mine = z * NC + c
    sends = [comm.send(mg, mg_in, mate)]
    for (kz, kc), p in zip(zc_offsets(), zc):
        slot = ((z + kz) % NZ) * NC + (c + kc) % NC
        sends.append(comm.send(pre.at[slot], pre_all.at[mine], p))
        sends.append(comm.send(cot.at[slot], cot_all.at[mine], p))
    sends.append(comm.send(txt, txt_in, mate))
    own = [
        pltpu.make_async_copy(pre.at[mine], pre_all.at[mine], ls.at[0]),
        pltpu.make_async_copy(cot.at[mine], cot_all.at[mine], ls.at[1]),
    ]
    for copy in own:
        copy.start()
    for copy in sends + own:
        copy.wait()


def weight_kernel(grad, out, x_in, y_out, y_in, z_out, ss, rs, ls):
    x, yl, z, c, t = coords()
    xs = [(dp_of((x + k) % NX, yl, z, c), t) for k in range(1, NX)]
    ys = (dp_of(x, 1 - yl, z, c), t)
    zc = zc_peers(x, yl, z, c, t)
    barrier(xs + [ys] + zc)
    comm = Comm(ss, rs)
    sends = [comm.send(grad.at[(x + k) % NX], x_in.at[k - 1], p) for k, p in zip(range(1, NX), xs)]
    for copy in sends:
        copy.wait()
    half = grad.shape[1] // 2

    def x_sum(side):
        rows = pl.ds(pl.multiple_of(side * half, half), half)
        total = grad[x, rows].astype(f32)
        for k in range(NX - 1):
            total = total + x_in[k, rows].astype(f32)
        return total

    y_out[...] = x_sum(1 - yl).astype(bf16)
    sent = comm.send(y_out, y_in, ys)
    z_out[...] = x_sum(yl)
    sent.wait()
    total = z_out[...] + y_in[...].astype(f32)
    mine = z * NC + c
    return total, mine, comm, zc


def weight_body(grad, out, x_in, y_out, y_in, z_out, blocks, ss, rs, ls):
    total, mine, comm, zc = weight_kernel(grad, out, x_in, y_out, y_in, z_out, ss, rs, ls)
    x, yl, z, c, t = coords()
    z_out[...] = total
    for i in range(NZ * NC):
        blocks[i, 0:26] = z_out[26 * i : 26 * i + 26]
        blocks[i, 26:32] = jnp.zeros((6, z_out.shape[1]), f32)
    sends = []
    for (kz, kc), p in zip(zc_offsets(), zc):
        slot = ((z + kz) % NZ) * NC + (c + kc) % NC
        sends.append(comm.send(blocks.at[slot], out.at[mine], p))
    out[mine] = blocks[mine]
    for copy in sends:
        copy.wait()


def unit_rows(values):
    floats = values.astype(jnp.float32)
    inverse = lax.rsqrt(jnp.sum(floats * floats, axis=1, keepdims=True) + 1e-06)
    return (floats * inverse, inverse)


def unit_back(normed, inverse, grad):
    return inverse * (grad - normed * jnp.sum(grad * normed, axis=1, keepdims=True))


def layer_norm(values):
    center = values - jnp.mean(values, axis=1, keepdims=True)
    scale_inv = lax.rsqrt(jnp.mean(center * center, axis=1, keepdims=True) + 1e-05)
    return (center * scale_inv, scale_inv)


def norm_back(grad, normed, scale_inv):
    return scale_inv * (
        grad
        - jnp.mean(grad, axis=1, keepdims=True)
        - normed * jnp.mean(grad * normed, axis=1, keepdims=True)
    )


def gelu_slope(values):
    return (
        0.5 * (1.0 + lax.erf(values * 0.7071067811865476))
        + values * jnp.exp(-0.5 * values * values) * 0.3989422804014327
    )


def contract_last(left, right):
    return lax.dot_general(
        left, right, (((1,), (1,)), ((), ())), preferred_element_type=jnp.float32
    )


def contract_first(left, right):
    return lax.dot_general(
        left, right, (((0,), (0,)), ((), ())), preferred_element_type=jnp.float32
    )


def shaped(shape, dtype):
    return jax.ShapeDtypeStruct(shape, dtype)


def local(image_cache, text_cache, labels, layer_input, ln1_gain, ln2_gain, w_up, w_down, proj):
    x, yl, z, c, t = coords()
    rows, embed = image_cache.shape
    width = layer_input.shape[1]
    half = rows // 2
    hidden = w_up.shape[1]
    hid = hidden // 8
    eh = embed // 2
    ec = eh // 8
    anys, vmem = pl.ANY, pltpu.VMEM

    img_norm, img_inv = unit_rows(image_cache)
    img_unit = img_norm.astype(bf16)
    txt_half = lax.dynamic_slice_in_dim(text_cache, t * half, half, 0)
    txt_norm, txt_inv = unit_rows(txt_half)
    txt_unit = txt_norm.astype(bf16)
    inputs = layer_input.astype(f32)
    normed_in, inv_in = layer_norm(inputs)
    mlp_in = (normed_in * ln1_gain).astype(bf16)
    pre = jnp.dot(mlp_in, w_up, preferred_element_type=f32)
    act = jax.nn.gelu(pre, approximate=False).astype(bf16)
    res_part = contract_last(act, w_down).astype(bf16)

    img_all, txt_all, lab_all, mlp_all, res_in = comm_call(
        gather_kernel,
        [
            shaped((NZ, rows, embed), bf16),
            shaped((NC, NX * NYL, half, embed), bf16),
            shaped((NZ, 1, rows), jnp.int32),
            shaped((NZ * NC, rows, width), bf16),
            shaped((rows, width), bf16),
        ],
        [anys] * 5,
        [anys] * 5,
        [],
        40,
        4,
        1,
        img_unit,
        txt_unit,
        labels.reshape(1, rows),
        mlp_in,
        res_part,
    )
    resid = inputs + (res_part.astype(f32) + res_in.astype(f32))
    normed_out, inv_out = layer_norm(resid)
    pooled = (normed_out * ln2_gain).astype(bf16)

    images = img_all.reshape(NZ * rows, embed)
    texts = txt_all.reshape(16 * half, embed)
    logits = logit_scale * contract_last(images, texts)
    row_peak = jnp.max(logits, axis=1)
    row_total = jnp.sum(jnp.exp(logits - row_peak[:, None]), axis=1)
    col_peak = jnp.max(logits, axis=0)
    col_total = jnp.sum(jnp.exp(logits - col_peak[None, :]), axis=0)
    n_row, n_col = row_peak.shape[0], col_peak.shape[0]
    row_stats = jnp.concatenate([row_peak, row_total]).reshape(2 * n_row // 128, 128)
    col_stats = jnp.concatenate([col_peak, col_total]).reshape(2 * n_col // 128, 128)
    rows_all, cols_all = comm_call(
        stats_kernel,
        [shaped((8,) + row_stats.shape, f32), shaped((16,) + col_stats.shape, f32)],
        [vmem] * 2,
        [vmem] * 2,
        [],
        22,
        1,
        2,
        row_stats,
        col_stats,
    )

    def total_of(stats, n):
        parts = stats.reshape(-1, 2, n)
        peak = jnp.max(parts[:, 0], axis=0)
        return peak + jnp.log(jnp.sum(parts[:, 1] * jnp.exp(parts[:, 0] - peak[None]), axis=0))

    row_lse = total_of(rows_all, n_row)
    col_lse = total_of(cols_all, n_col)
    place = jnp.arange(n_col, dtype=jnp.int32)
    slot = place // half
    text_index = (
        ((slot % (NX * NYL)) * NZ + z) * NC + slot // (NX * NYL)
    ) * rows + t * half + place % half
    match = (lab_all.reshape(n_row)[:, None] == text_index[None, :]).astype(f32)
    grad = (
        0.5 * (jnp.exp(logits - row_lse[:, None]) + jnp.exp(logits - col_lse[None, :])) - match
    ).astype(bf16)
    part_img = (logit_scale * jnp.dot(grad, texts, preferred_element_type=f32)).astype(bf16)
    part_txt = (logit_scale * contract_first(grad, images)).astype(bf16)

    img_two, txt_sum, pooled_all = comm_call(
        reduce_kernel,
        [
            shaped((2, rows, embed), bf16),
            shaped((half, embed), f32),
            shaped((NZ * NC, rows, width), bf16),
        ],
        [vmem, vmem, anys],
        [vmem, vmem, anys],
        [
            pltpu.VMEM((NZ - 1, rows, embed), bf16),
            pltpu.VMEM((NX * NYL, half, embed), bf16),
            pltpu.VMEM((NX * NYL - 1, half, embed), bf16),
            pltpu.VMEM((NX * NYL - 1, half, embed), bf16),
        ],
        24,
        1,
        3,
        part_img.reshape(NZ, rows, embed),
        part_txt.reshape(NC, NX * NYL, half, embed),
        pooled,
    )
    img_unit_grad = img_two[0].astype(f32) + img_two[1].astype(f32)
    image_grad = unit_back(img_norm, img_inv, img_unit_grad)
    text_half = unit_back(txt_norm, txt_inv, txt_sum).astype(bf16)
    cotangent = image_grad.astype(bf16)
    pooled_grad = contract_last(cotangent, proj)
    resid_grad = norm_back(pooled_grad * ln2_gain, normed_out, inv_out)
    resid_cot = resid_grad.astype(bf16)
    pre_grad = (jnp.dot(resid_cot, w_down, preferred_element_type=f32) * gelu_slope(pre)).astype(
        bf16
    )
    mg_part = contract_last(pre_grad, w_up).astype(bf16)
    cot_half = lax.dynamic_slice_in_dim(cotangent, t * eh, eh, 1)

    pre_all, cot_all, mg_in, txt_in = comm_call(
        swap_kernel,
        [
            shaped((8, rows, hid), bf16),
            shaped((8, ec, rows), bf16),
            shaped((rows, width), bf16),
            shaped((half, embed), bf16),
        ],
        [anys] * 4,
        [anys] * 4,
        [],
        16,
        2,
        4,
        pre_grad.reshape(rows, 8, hid).transpose(1, 0, 2),
        cot_half.T.reshape(8, ec, rows),
        mg_part,
        text_half,
    )
    mlp_in_grad = mg_part.astype(f32) + mg_in.astype(f32)
    input_grad = (resid_grad + norm_back(mlp_in_grad * ln1_gain, normed_in, inv_in)).astype(bf16)
    text_grad = jnp.where(
        t == 0,
        jnp.concatenate([text_half, txt_in], axis=0),
        jnp.concatenate([txt_in, text_half], axis=0),
    )
    up_part = contract_first(mlp_all.reshape(8 * rows, width), pre_all.reshape(8 * rows, hid))
    cots = jnp.pad(cot_all, ((0, 0), (0, 128 - ec), (0, 0)))
    proj_part = lax.dot_general(
        pooled_all.reshape(8 * rows, width),
        cots.transpose(0, 2, 1).reshape(8 * rows, 128),
        (((0,), (0,)), ((), ())),
        preferred_element_type=f32,
    )
    both = jnp.concatenate([up_part, proj_part], axis=1).astype(bf16)
    cols = hid + 128
    quarter = width // NX
    (summed,) = comm_call(
        weight_body,
        [shaped((8, 32, cols), f32)],
        [vmem],
        [vmem],
        [
            pltpu.VMEM((NX - 1, quarter, cols), bf16),
            pltpu.VMEM((quarter // 2, cols), bf16),
            pltpu.VMEM((quarter // 2, cols), bf16),
            pltpu.VMEM((quarter // 2, cols), f32),
            pltpu.VMEM((8, 32, cols), f32),
        ],
        12,
        1,
        5,
        both.reshape(NX, quarter, cols),
    )
    share = width // 64
    up_grad = summed[:, :share, :hid].transpose(1, 0, 2).reshape(share, hidden)
    proj_grad = summed[:, :share, hid : hid + ec].transpose(1, 0, 2).reshape(share, eh)
    return (text_grad, input_grad, up_grad, proj_grad)


def solution(mesh):
    in_specs = (
        P("dp", None),
        P("dp", None),
        P("dp"),
        P("dp", None),
        P(),
        P(),
        P(None, "tensor"),
        P(None, "tensor"),
        P(),
    )
    out_specs = (P("dp", None), P("dp", None), P("dp", "tensor"), P("dp", "tensor"))
    return jax.shard_map(local, mesh=mesh, in_specs=in_specs, out_specs=out_specs, check_vma=False)
```

time: 1380 us -> 194 us (0.14)
  waiting for transfers between devices: 692 us -> 0 us
  blocking collectives: 575 us -> 0 us
  Pallas kernels: 0 us -> 141 us
  matrix products: 54.5 us -> 32.5 us
  between operations: 15.5 us -> 1.18 us
    unnamed x6 -> x0, waiting for transfers between devices: 598 us -> none
    unnamed x2 -> x0, blocking collectives: 557 us -> none
    pallas_call x0 -> x5, Pallas kernels: none -> 141 us  [comm_call(): pl.pallas_call(kernel, out_shape=out_shapes, in_specs=[pl.BlockSpec(memor...]
    psum x2 -> x0, waiting for transfers between devices: 94.1 us -> none  [the longest x1 75 us: local(): img_unit_grad, txt_unit_grad = lax.psum((part_img, part_txt), 'tensor')]
    all_gather x4 -> x0, blocking collectives: 18.4 us -> none  [combined_all(): gathered = jax.tree.map(lambda a: lax.all_gather(a, axis), part)]
  transfers between devices with their start and end apart: 5 -> 0, of which waited for: 3 -> 0; matrix products, arithmetic and copies ran while one was open for 3% -> 0% of each run, Pallas kernels for 0% -> 0%
where the time goes in v1:
time: 194 us; the launch traced here: 193 us
  Pallas kernels  141 us (73%)
  matrix products  32.5 us (17%)
  other arithmetic  13.6 us (7%)
  local copies, waits for them, and re-layouts  5.19 us (3%)
    pallas_call x5, Pallas kernels, comm_call(): pl.pallas_call(kernel, out_shape=out_shapes, in_specs=[pl.BlockSpec(memor...  141 us
    dot_general x4, matrix products, contract_last(): lax.dot_general(left, right, (((1,), (1,)), ((), ())), preferred_element_...  17 us
    dot_general x1, matrix products, local(): jnp.dot(grad, texts, preferred_element_type=f32)  4.59 us
    dot_general x1, matrix products, local(): pre = jnp.dot(mlp_in, w_up, preferred_element_type=f32)  4.21 us

profile of v1, /device:TPU:1, one launch (start us, length us, event | category | flops | bytes accessed | tf_op | source)
XLA Modules:
  0.0 193.4 jit_solution(17393130826116764825)
XLA Ops:
  0.6 1.1 convert_reduce_fusion
  1.8 1.3 fusion.29
  3.1 1.3 fusion.23.mlp
  4.4 0.0 copy-start.7
  4.4 0.0 copy-start.12
  4.4 4.2 %fusion.146 = f32[128,2048]{1,0:T(8,128)S(1)} fusion(bf16[128,1664]{1,0:T(8,128)(2,1)S(1)} %fusion.23.mlp, bf16[1664,2048]{1,0:T(8,128)(2,1)} %param.15), kind=kOutput, calls=%fused_computation.213 | convolution fusion | flops 872415232 | bytes 8290304 | tf_op jit(solution)/shard_map/dot_general | solution.py:333
  8.6 0.0 copy-done.7
  8.6 0.0 copy-start.14
  8.6 0.1 fusion.37
  8.8 0.1 fusion.32.img
  8.9 0.0 copy-done.12
  9.0 0.1 fusion.78
  9.1 0.1 fusion.73.txt
  9.2 0.5 copy-done.14
  9.7 7.1 %convolution_convert_fusion.1.res = bf16[128,1664]{1,0:T(8,128)(2,1)S(1)} fusion(bf16[1664,2048]{1,0:T(8,128)(2,1)} %param.16, f32[128,2048]{1,0:T(8,128)S(1)} %fusion.146), kind=kOutput, calls=%fused_computation.11 | convolution fusion | flops 889667584 | bytes 8290304 | tf_op jit(solution)/shard_map/dot_general | solution.py:299
  16.8 0.0 copy-done
  16.8 46.4 %shard_map.120 = (bf16[4,128,1280]{2,1,0:T(8,128)(2,1)S(1)}, bf16[2,8,64,1280]{3,2,1,0:T(8,128)(2,1)S(1)}, s32[4,1,128]{2,1,0:T(1,128)S(1)}, bf16[8,128,1664]{2,1,0:T(8,128)(2,1)S(1)}, bf16[128,1664]{1,0:T(8,128)(2,1)S(1)}) custom-call(bf16[128,1280]{1,0:T(8,128)(2,1)S(1)} %fusion.32.img, bf16[64,1280]{1,0:T(8,128)(2,1)S(1)} %fusion.73.txt, ...), custom_call_target="tpu_custom_call" | custom-call | tf_op jit(solution)/shard_map/pallas_call | solution.py:55
  63.2 0.0 copy-start.1
  63.3 0.2 fusion.141
  63.5 0.3 multiply_reduce_fusion.1
  63.8 2.9 %fusion.142 = (f32[1024]{0:T(1024)S(1)}, f32[512]{0:T(512)S(1)}, f32[512,1024]{1,0:T(8,128)}) fusion(bf16[512,1280]{1,0:T(8,128)(2,1)S(1)} %bitcast.84, bf16[1024,1280]{1,0:T(8,128)(2,1)S(1)} %bitcast.82), kind=kOutput, calls=%fused_computation.209 | convolution fusion | flops 1343748608 | bytes 6035456 | tf_op jit(solution)/shard_map/dot_general | solution.py:299
  66.7 2.3 %exponential_reduce_fusion = (f32[1024]{0:T(1024)S(1)}, f32[512]{0:T(512)S(1)}) fusion(f32[512,1024]{1,0:T(8,128)} %get-tuple-element.46, f32[1024]{0:T(1024)S(1)} %get-tuple-element.34, f32[512]{0:T(512)S(1)} %get-tuple-element.35), kind=kLoop, calls=%fused_computation.13 | loop fusion | flops 2095616 | bytes 2109440 | tf_op jit(solution)/shard_map/reduce_sum | solution.py:368
  69.1 7.3 %shard_map.121 = (f32[8,8,128]{2,1,0:T(8,128)S(1)}, f32[16,16,128]{2,1,0:T(8,128)S(1)}) custom-call(f32[8,128]{1,0:T(8,128)S(1)} %pad_maximum_fusion.2.rows, f32[16,128]{1,0:T(8,128)S(1)} %pad_maximum_fusion.1.cols), custom_call_target="tpu_custom_call" | custom-call | tf_op jit(solution)/shard_map/pallas_call | solution.py:55
  76.4 0.1 reshape.189
  76.5 0.1 fusion.144
  76.8 0.0 slice-start
  76.8 0.0 slice-start.2
  76.8 4.6 %fusion = bf16[512,1280]{1,0:T(8,128)(2,1)S(1)} fusion(bf16[1024,1280]{1,0:T(8,128)(2,1)} %bitcast.83, f32[512,1024]{1,0:T(8,128)} %get-tuple-element.46, s32[1024]{0:T(1024)S(1)} %fusion.101, f32[1024]{0:T(1024)S(1)} %log_add_fusion, f32[512]{0:T(512)S(1)} %log_add_fusion.1, s32[512]{0:T(512)S(1)} %bitcast.86), kind=kOutput, calls=%fused_computation.2 | convolution fusion | flops 1347682304 | bytes 6041600 | tf_op jit(solution)/shard_map/dot_general | solution.py:401
  81.4 0.0 copy-start.17
  81.4 0.0 slice-start.1
  81.4 0.0 slice-start.3
  81.5 2.0 %multiply_convert_fusion = bf16[1024,1280]{1,0:T(8,128)(2,1)S(1)} fusion(bf16[512,1280]{1,0:T(8,128)(2,1)S(1)} %bitcast.85, f32[512,1024]{1,0:T(8,128)S(1)} %copy-done.11, s32[1024]{0:T(1024)S(1)} %fusion.101, f32[1024]{0:T(1024)S(1)} %log_add_fusion, f32[512]{0:T(512)S(1)} %log_add_fusion.1, s32[512]{0:T(512)S(1)} %bitcast.87), kind=kOutput, calls=%fused_computation | convolution fusion | flops 1348993024 | bytes 6041600 | tf_op jit(solution)/shard_map/dot_general | solution.py:305
  83.5 0.3 multiply_convert_fusion.1.pooled
  83.8 0.0 copy-start.8
  83.8 41.5 %shard_map.122 = (bf16[2,128,1280]{2,1,0:T(8,128)(2,1)S(1)}, f32[64,1280]{1,0:T(8,128)S(1)}, bf16[8,128,1664]{2,1,0:T(8,128)(2,1)S(1)}) custom-call(bf16[4,128,1280]{2,1,0:T(8,128)(2,1)S(1)} %bitcast.79, bf16[2,8,64,1280]{3,2,1,0:T(8,128)(2,1)S(1)} %bitcast.77, bf16[128,1664]{1,0:T(8,128)(2,1)S(1)} %multiply_convert_fusion.1.pooled), custom_call_target="tpu_custom_call" | custom-call | tf_op jit(solution)/shard_map/pallas_call | solution.py:55
  125.3 0.0 copy-start.3
  125.3 0.0 copy-done.8
  125.3 0.3 fusion.33
  125.6 0.3 fusion.36
  125.9 0.0 copy-start.15
  125.9 1.6 fusion.143
  127.5 0.2 copy-done.15
  127.7 2.5 %fusion.2 = bf16[128,2048]{1,0:T(8,128)(2,1)} fusion(bf16[1664,2048]{1,0:T(8,128)(2,1)S(1)} %bitcast.100, f32[128,2048]{1,0:T(8,128)S(1)} %copy-done.15, f32[128,1664]{1,0:T(8,128)S(1)} %get-tuple-element.47, f32[128]{0:T(128)S(1)} %get-tuple-element.48, f32[128]{0:T(128)S(1)} %get-tuple-element.49, f32[128]{0:T(128)S(1)} %add_rsqrt_fusion, ...), kind=kOutput, calls=%fused_computation.8 | convolution fusion | flops 877592576 | bytes 10520576 | tf_op jit(solution)/shard_map/dot_general | solution.py:433
  130.2 1.3 copy.21
  131.5 0.2 copy.22
  131.8 0.2 copy.23
  132.0 5.5 %convolution_convert_fusion.mg = bf16[128,1664]{1,0:T(8,128)(2,1)S(1)} fusion(bf16[128,2048]{1,0:T(8,128)(2,1)} %fusion.2, bf16[1664,2048]{1,0:T(8,128)(2,1)} %param.15), kind=kOutput, calls=%fused_computation.10 | convolution fusion | flops 872628224 | bytes 7766016 | tf_op jit(solution)/shard_map/dot_general | solution.py:299
  137.4 0.0 copy-start.16
  137.4 0.0 copy-done.13
  137.4 0.2 fusion.74
  137.7 0.1 fusion.77.txt
  137.8 16.7 %shard_map.123 = (bf16[8,128,256]{2,1,0:T(8,128)(2,1)S(1)}, bf16[8,80,128]{2,1,0:T(8,128)(2,1)S(1)}, bf16[128,1664]{1,0:T(8,128)(2,1)S(1)}, bf16[64,1280]{1,0:T(8,128)(2,1)S(1)}) custom-call(bf16[8,128,256]{2,1,0:T(8,128)(2,1)S(1)} %bitcast.78, bf16[8,80,128]{2,1,0:T(8,128)(2,1)S(1)} %bitcast.80, bf16[128,1664]{1,0:T(8,128)(2,1)S(1)} %convolution_convert_fusion.mg, ...), custom_call_target="tpu_custom_call" | custom-call | tf_op jit(solution)/shard_map/pallas_call | solution.py:55
  154.5 0.8 maximum_select_fusion
  155.3 1.5 fusion.38
  156.9 2.6 %fusion.28 = bf16[128,1664]{1,0:T(8,128)(2,1)} fusion(bf16[128,1664]{1,0:T(8,128)(2,1)} %param.12, bf16[128,1664]{1,0:T(8,128)(2,1)S(1)} %get-tuple-element.27, bf16[128,1664]{1,0:T(8,128)(2,1)S(1)} %convolution_convert_fusion.mg, f32[128]{0:T(128)S(1)} %broadcast_multiply_fusion, f32[128]{0:T(128)S(1)} %broadcast_multiply_fusion.1, f32[1664]{0:T(1024)S(1)} %copy-done.16, ...), kind=kLoop, calls=%fused_computation.54 | loop fusion | flops 4898816 | bytes 3418624 | tf_op jit(solution)/shard_map/convert_element_type | solution.py:459
  159.5 1.1 fusion.3
  160.6 0.8 copy-done.2
  161.4 1.1 fusion.1
  162.6 0.1 pad_maximum_fusion.grad
  162.7 28.9 %shard_map.124 = f32[8,32,384]{2,1,0:T(8,128)S(1)} custom-call(bf16[4,416,384]{2,1,0:T(8,128)(2,1)S(1)} %pad_maximum_fusion.grad), custom_call_target="tpu_custom_call" | custom-call | tf_op jit(solution)/shard_map/pallas_call | solution.py:55
  191.6 0.1 copy.27
  191.8 0.8 copy.38
  192.6 0.1 copy.28
  192.6 0.7 reshape.195
  (47 shorter events, 0.3 us)
Async XLA Ops:
  4.4 4.2 %copy-start.7 = (bf16[128,1280]{1,0:T(8,128)(2,1)S(1)}, bf16[128,1280]{1,0:T(8,128)(2,1)}, u32[]{:S(2)}) copy-start(bf16[128,1280]{1,0:T(8,128)(2,1)} %param.9) | copy-start | bytes 983044
  4.4 4.5 %copy-start.12 = (bf16[128,1280]{1,0:T(8,128)(2,1)S(1)}, bf16[128,1280]{1,0:T(8,128)(2,1)}, u32[]{:S(2)}) copy-start(bf16[128,1280]{1,0:T(8,128)(2,1)} %param.10) | copy-start | bytes 983044
  8.6 1.0 copy-start.14
  9.7 7.1 %copy-start = (s32[128]{0:T(128)S(1)}, s32[128]{0:T(128)}, u32[]{:S(2)}) copy-start(s32[128]{0:T(128)} %param.11) | copy-start | bytes 1540
  9.7 53.6 %copy-start.6 = (bf16[128,1664]{1,0:T(8,128)(2,1)S(1)}, bf16[128,1664]{1,0:T(8,128)(2,1)}, u32[]{:S(2)}) copy-start(bf16[128,1664]{1,0:T(8,128)(2,1)} %param.12) | copy-start | bytes 1277956
  63.2 3.5 %copy-start.1 = (bf16[8,128,1664]{2,1,0:T(8,128)(2,1)}, bf16[8,128,1664]{2,1,0:T(8,128)(2,1)S(1)}, u32[]{:S(2)}) copy-start(bf16[8,128,1664]{2,1,0:T(8,128)(2,1)S(1)} %get-tuple-element.28) | copy-start | bytes 10223620
  63.2 3.5 %copy-start.5 = (bf16[2,8,64,1280]{3,2,1,0:T(8,128)(2,1)}, bf16[2,8,64,1280]{3,2,1,0:T(8,128)(2,1)S(1)}, u32[]{:S(2)}) copy-start(bf16[2,8,64,1280]{3,2,1,0:T(8,128)(2,1)S(1)} %get-tuple-element.19) | copy-start | bytes 7864324
  76.8 4.6 %copy-start.11 = (f32[512,1024]{1,0:T(8,128)S(1)}, f32[512,1024]{1,0:T(8,128)}, u32[]{:S(2)}) copy-start(f32[512,1024]{1,0:T(8,128)} %get-tuple-element.46) | copy-start | bytes 6291460
  76.8 49.1 %slice-start = ((s8[4259840]{0:T(1024)(128)(4,1)}), s8[4194304]{0:T(1024)(128)(4,1)S(1)}, s32[]{:S(2)}) async-start(s8[4259840]{0:T(1024)(128)(4,1)} %bitcast.88), calls=%async_computation | async-start | bytes 8388608
  76.8 50.7 %slice-start.2 = ((s8[6815744]{0:T(1024)(128)(4,1)}), s8[4194304]{0:T(1024)(128)(4,1)S(1)}, s32[]{:S(2)}) async-start(s8[6815744]{0:T(1024)(128)(4,1)} %bitcast.99), calls=%async_computation.2 | async-start | bytes 8388608
  81.4 2.1 %copy-start.17 = (f32[1664]{0:T(1024)S(1)}, f32[1664]{0:T(1024)}, u32[]{:S(2)}) copy-start(f32[1664]{0:T(1024)} %param.14) | copy-start | bytes 19972
  81.4 44.4 %slice-start.1 = ((s8[4259840]{0:T(1024)(128)(4,1)}), s8[65536]{0:T(1024)(128)(4,1)S(1)}, s32[]{:S(2)}) async-start(s8[4259840]{0:T(1024)(128)(4,1)} %bitcast.88), calls=%async_computation.1 | async-start | bytes 131072
  81.4 46.1 %slice-start.3 = ((s8[6815744]{0:T(1024)(128)(4,1)}), s8[2621440]{0:T(1024)(128)(4,1)S(1)}, s32[]{:S(2)}) async-start(s8[6815744]{0:T(1024)(128)(4,1)} %bitcast.99), calls=%async_computation.3 | async-start | bytes 5242880
  83.8 41.5 %copy-start.8 = (bf16[128,1280]{1,0:T(8,128)(2,1)S(1)}, bf16[128,1280]{1,0:T(8,128)(2,1)}, u32[]{:S(2)}) copy-start(bf16[128,1280]{1,0:T(8,128)(2,1)} %param.9) | copy-start | bytes 983044
  125.3 2.2 %copy-start.3 = (bf16[8,128,1664]{2,1,0:T(8,128)(2,1)}, bf16[8,128,1664]{2,1,0:T(8,128)(2,1)S(1)}, u32[]{:S(2)}) copy-start(bf16[8,128,1664]{2,1,0:T(8,128)(2,1)S(1)} %get-tuple-element.30) | copy-start | bytes 10223620
  125.9 1.8 copy-start.15
  127.5 2.7 %copy-start.9 = (f32[128,1664]{1,0:T(8,128)}, f32[128,1664]{1,0:T(8,128)S(1)}, u32[]{:S(2)}) copy-start(f32[128,1664]{1,0:T(8,128)S(1)} %get-tuple-element.47) | copy-start | bytes 2555908
  132.0 5.5 %copy-start.13 = (bf16[128,1280]{1,0:T(8,128)(2,1)S(1)}, bf16[128,1280]{1,0:T(8,128)(2,1)}, u32[]{:S(2)}) copy-start(bf16[128,1280]{1,0:T(8,128)(2,1)} %param.10) | copy-start | bytes 983044
  137.4 17.9 %copy-start.16 = (f32[1664]{0:T(1024)S(1)}, f32[1664]{0:T(1024)}, u32[]{:S(2)}) copy-start(f32[1664]{0:T(1024)} %param.13) | copy-start | bytes 19972
  154.5 2.3 %copy-start.10 = (f32[128,1664]{1,0:T(8,128)S(1)}, f32[128,1664]{1,0:T(8,128)}, u32[]{:S(2)}) copy-start(f32[128,1664]{1,0:T(8,128)} %copy-done.9) | copy-start | bytes 2555908
  155.3 4.1 %copy-start.4 = (bf16[8,128,1664]{2,1,0:T(8,128)(2,1)S(1)}, bf16[8,128,1664]{2,1,0:T(8,128)(2,1)}, u32[]{:S(2)}) copy-start(bf16[8,128,1664]{2,1,0:T(8,128)(2,1)} %copy-done.3) | copy-start | bytes 10223620
  159.5 2.0 %copy-start.2 = (bf16[8,128,1664]{2,1,0:T(8,128)(2,1)S(1)}, bf16[8,128,1664]{2,1,0:T(8,128)(2,1)}, u32[]{:S(2)}) copy-start(bf16[8,128,1664]{2,1,0:T(8,128)(2,1)} %copy-done.1) | copy-start | bytes 10223620

commit v2 on v0

v2 whole, which is shorter than its diff:
```python
import jax
import jax.numpy as jnp
from jax import lax
from jax.experimental import pallas as pl
from jax.experimental.pallas import tpu as pltpu
from jax.sharding import PartitionSpec as P

logit_scale = 100.0
MESH = pl.DeviceIdType.MESH
NX, NYL, NZ, NC = 4, 2, 4, 2
bf16 = jnp.bfloat16
f32 = jnp.float32
VMEM_LIMIT = 60 * 1024 * 1024


def dp_of(x, yl, z, c):
    return ((x * NYL + yl) * NZ + z) * NC + c


def coords():
    d = lax.axis_index("dp")
    c = d % NC
    z = (d // NC) % NZ
    yl = (d // (NC * NZ)) % NYL
    x = d // (NC * NZ * NYL)
    return x, yl, z, c, lax.axis_index("tensor")


class Comm:
    def __init__(self, send_sem, recv_sem):
        self.send_sem, self.recv_sem, self.n = send_sem, recv_sem, 0

    def send(self, src, dst, dev):
        i = self.n
        self.n += 1
        copy = pltpu.make_async_remote_copy(
            src_ref=src,
            dst_ref=dst,
            send_sem=self.send_sem.at[i],
            recv_sem=self.recv_sem.at[i],
            device_id=dev,
            device_id_type=MESH,
        )
        copy.start()
        return copy


def z_offsets():
    return list(range(1, NZ))


def zc_offsets():
    return [(kz, kc) for kz in range(NZ) for kc in range(NC) if (kz, kc) != (0, 0)]


def unit_rows(values):
    floats = values.astype(f32)
    inverse = lax.rsqrt(jnp.sum(floats * floats, axis=1, keepdims=True) + 1e-06)
    return (floats * inverse, inverse)


def unit_back(normed, inverse, grad):
    return inverse * (grad - normed * jnp.sum(grad * normed, axis=1, keepdims=True))


def layer_norm(values):
    center = values - jnp.mean(values, axis=1, keepdims=True)
    scale_inv = lax.rsqrt(jnp.mean(center * center, axis=1, keepdims=True) + 1e-05)
    return (center * scale_inv, scale_inv)


def norm_back(grad, normed, scale_inv):
    return scale_inv * (
        grad
        - jnp.mean(grad, axis=1, keepdims=True)
        - normed * jnp.mean(grad * normed, axis=1, keepdims=True)
    )


def contract_last(left, right):
    return lax.dot_general(left, right, (((1,), (1,)), ((), ())), preferred_element_type=f32)


def dot(left, right):
    return jnp.dot(left, right, preferred_element_type=f32)


def at(index, size):
    return pl.ds(pl.multiple_of(index * size, size), size)


def chunks(total, size):
    return [(i, min(size, total - i)) for i in range(0, total, size)]


def to_column(row, n):
    return jnp.transpose(jnp.broadcast_to(row, (128, n)))[:, 0:1]


def to_row(column, n):
    return jnp.transpose(jnp.broadcast_to(column, (n, 128)))[0:1]


def merged_lse(parts, count):
    peak = parts[0, 0:1]
    for i in range(1, count):
        peak = jnp.maximum(peak, parts[i, 0:1])
    total = jnp.zeros_like(peak)
    for i in range(count):
        total = total + parts[i, 1:2] * jnp.exp(parts[i, 0:1] - peak)
    return peak + jnp.log(total)


def body(
    img_ref, txt_ref, lab_ref, lin_ref, g1_ref, g2_ref, up_hbm, down_hbm, proj_hbm,
    text_out, input_out, up_out, proj_out,
    w_up, w_down, w_proj, img_all, txt_all, lab_all, mlp_t, pooled_t, act, slope,
    res_out, res_in, n_in, n_out, logits, row_st, col_st, rows_all, cols_all,
    grad, grad_t, pimg, img_in, img_sum, img_mate, ptxt, sib_in, txo, txi, tyo, tyi, tsum,
    rgrad, cot_t, cot_all, pre_out, pre_all, mg_out, mg_in,
    wp, wu, wpi, wui, wyo, wyi, wsum, wblk_u, wblk_p,
    ss, rs, ls,
):
    x, yl, z, c, t = coords()
    me = lax.axis_index("dp")
    rows, embed = img_ref.shape
    width = lin_ref.shape[1]
    half = rows // 2
    hidden = up_hbm.shape[1]
    hid = hidden // 8
    eh = embed // 2
    ec = eh // 8
    sib, mate, ynb = (dp_of(x, yl, z, 1 - c), t), (me, 1 - t), (dp_of(x, 1 - yl, z, c), t)
    zp = [(dp_of(x, yl, (z + k) % NZ, c), t) for k in range(1, NZ)]
    xp = [(dp_of((x + k) % NX, yl, z, c), t) for k in range(1, NX)]
    zc = [(dp_of(x, yl, (z + kz) % NZ, (c + kc) % NC), t) for kz, kc in zc_offsets()]
    row_peers = [
        (dp_of(x, yl, (z + k) % NZ, c), (t + j) % 2) for k in range(NZ) for j in range(2) if k or j
    ]
    col_peers = [
        (dp_of((x + kx) % NX, (yl + ky) % NYL, z, (c + kc) % NC), t)
        for kx in range(NX)
        for ky in range(NYL)
        for kc in range(NC)
        if kx or ky or kc
    ]
    cross = [p for (kz, kc), p in zip(zc_offsets(), zc) if kz and kc]
    greet = row_peers + col_peers + cross
    entry = pltpu.get_barrier_semaphore()
    for peer in greet:
        pl.semaphore_signal(entry, inc=1, device_id=peer, device_id_type=MESH)
    loads = [
        pltpu.make_async_copy(up_hbm, w_up, ls.at[0]),
        pltpu.make_async_copy(down_hbm, w_down, ls.at[1]),
        pltpu.make_async_copy(proj_hbm, w_proj, ls.at[2]),
    ]
    for copy in loads:
        copy.start()
    my_slot = c * 8 + x * NYL + yl
    img_unit, _ = unit_rows(img_ref[...])
    img_all[at(z, rows)] = img_unit.astype(bf16)
    txt_unit, _ = unit_rows(txt_ref[at(t, half)])
    txt_all[at(my_slot, half)] = txt_unit.astype(bf16)
    lab_all[z] = lab_ref[...]
    cot_all[ec:] = jnp.zeros((128 - ec, 8 * rows), bf16)
    pl.semaphore_wait(entry, len(greet))

    comm = Comm(ss, rs)
    send = comm.send

    def same(ref, index, size, dev):
        return send(ref.at[at(index, size)], ref.at[at(index, size)], dev)

    t_y = same(txt_all, my_slot, half, ynb)
    t_x = [same(txt_all, my_slot, half, p) for p in xp]
    i_z = [same(img_all, z, rows, p) for p in zp]
    l_z = [send(lab_all.at[z], lab_all.at[z], p) for p in zp]
    t_s = [same(txt_all, my_slot, half, sib)]

    inputs = lin_ref[...].astype(f32)
    normed_in, inv_in = layer_norm(inputs)
    n_in[...] = normed_in
    mlp_f = n_in[...] * g1_ref[...]
    mlp_in = mlp_f.astype(bf16)
    my_zc = z * NC + c
    for i, n in chunks(width, 128):
        mlp_t[i : i + n, at(my_zc, 128)] = jnp.transpose(
            n_in[:, i : i + n] * g1_ref[:, i : i + n]
        ).astype(bf16)
    t_y.wait_recv()
    other = c * 8 + x * NYL + (1 - yl)
    f_x = [same(txt_all, other, half, p) for p in xp]
    t_s.append(same(txt_all, other, half, sib))

    loads[0].wait()

    def up_tile(i, _):
        cols = at(i, 256)
        pre = dot(mlp_in, w_up[:, cols])
        phi = 0.5 * (1.0 + lax.erf(pre * 0.7071067811865476))
        act[:, cols] = (pre * phi).astype(bf16)
        slope[:, cols] = phi + pre * jnp.exp(-0.5 * pre * pre) * 0.3989422804014327
        return _

    lax.fori_loop(0, hidden // 256, up_tile, 0)
    for k, copy in zip(range(1, NX), t_x):
        copy.wait_recv()
        t_s.append(same(txt_all, c * 8 + ((x + NX - k) % NX) * NYL + yl, half, sib))
    loads[1].wait()
    acts = act[...]
    for i, n in chunks(width, 256):
        res_out[:, i : i + n] = contract_last(acts, w_down[i : i + n]).astype(bf16)
    res_c = send(res_out, res_in, mate)
    for k, copy in zip(range(1, NX), f_x):
        copy.wait_recv()
        t_s.append(same(txt_all, c * 8 + ((x + NX - k) % NX) * NYL + (1 - yl), half, sib))
    for copy in i_z + l_z:
        copy.wait()
    m_z = [
        send(mlp_t.at[:, at(my_zc, 128)], mlp_t.at[:, at(my_zc, 128)], p) for p in zp
    ]
    for copy in t_s:
        copy.wait()
    t_y.wait_send()
    for copy in t_x + f_x:
        copy.wait_send()

    n_row, n_col = img_all.shape[0], txt_all.shape[0]
    tile = 256

    def logit_tile(i, peak):
        tile_logits = logit_scale * contract_last(img_all[...], txt_all[at(i, tile)])
        logits[:, at(i, tile)] = tile_logits
        return jnp.maximum(peak, jnp.max(tile_logits, axis=1, keepdims=True))

    row_peak = lax.fori_loop(
        0, n_col // tile, logit_tile, jnp.full((n_row, 1), -jnp.inf, f32)
    )

    def total_tile(i, total):
        cols = at(i, tile)
        part = logits[:, cols]
        col_peak = jnp.max(part, axis=0, keepdims=True)
        col_st[0:1, cols] = col_peak
        col_st[1:2, cols] = jnp.sum(jnp.exp(part - col_peak), axis=0, keepdims=True)
        return total + jnp.sum(jnp.exp(part - row_peak), axis=1, keepdims=True)

    row_total = lax.fori_loop(0, n_col // tile, total_tile, jnp.zeros((n_row, 1), f32))
    my_col, my_row = (x * NYL + yl) * NC + c, z * 2 + t
    stats = [send(col_st, cols_all.at[my_col], p) for p in col_peers]
    row_st[0:1] = to_row(row_peak, n_row)
    row_st[1:2] = to_row(row_total, n_row)
    stats += [send(row_st, rows_all.at[my_row], p) for p in row_peers]
    rows_all[my_row] = row_st[...]
    cols_all[my_col] = col_st[...]

    res_c.wait()
    resid = lin_ref[...].astype(f32) + (res_out[...].astype(f32) + res_in[...].astype(f32))
    normed_out, inv_out = layer_norm(resid)
    n_out[...] = normed_out
    for i, n in chunks(width, 128):
        pooled_t[i : i + n, at(my_zc, 128)] = jnp.transpose(
            n_out[:, i : i + n] * g2_ref[:, i : i + n]
        ).astype(bf16)
    for copy in stats:
        copy.wait()

    row_lse = to_column(merged_lse(rows_all, 8), n_row)
    col_st[0:1] = merged_lse(cols_all, 16)
    label_col = jnp.concatenate(
        [to_column(lab_all[i, 0:1].astype(f32), rows) for i in range(NZ)], axis=0
    )

    def grad_tile(i, _):
        cols = at(i, tile)
        part = logits[:, cols]
        place = i * tile + lax.broadcasted_iota(jnp.int32, (1, tile), 1)
        slot = place // half
        index = (((slot % (NX * NYL)) * NZ + z) * NC + slot // (NX * NYL)) * rows
        index = (index + t * half + place % half).astype(f32)
        value = 0.5 * (jnp.exp(part - row_lse) + jnp.exp(part - col_st[0:1, cols]))
        value = value - jnp.where(label_col == index, 1.0, 0.0)
        grad[:, cols] = value.astype(bf16)
        grad_t[at(i, tile)] = jnp.transpose(value).astype(bf16)
        return _

    lax.fori_loop(0, n_col // tile, grad_tile, 0)

    def img_tile(i, _):
        cols = at(i, 256)
        pimg[:, cols] = (logit_scale * dot(grad[...], txt_all[:, cols])).astype(bf16)
        return _

    lax.fori_loop(0, embed // 256, img_tile, 0)
    r_z = [
        send(pimg.at[at((z + k) % NZ, rows)], img_in.at[k - 1], p)
        for k, p in zip(range(1, NZ), zp)
    ]

    def txt_tile(i, _):
        cols = at(i, 256)
        ptxt[:, cols] = (logit_scale * dot(grad_t[...], img_all[:, cols])).astype(bf16)
        return _

    lax.fori_loop(0, embed // 256, txt_tile, 0)
    side = 8 * half
    to_sib = send(ptxt.at[at(1 - c, side)], sib_in, sib)
    m_s = [send(mlp_t.at[:, at(my_zc, 128)], mlp_t.at[:, at(my_zc, 128)], sib)]
    for k, copy in zip(range(1, NZ), m_z):
        copy.wait_recv()
        cols = at(((z + NZ - k) % NZ) * NC + c, 128)
        m_s.append(send(mlp_t.at[:, cols], mlp_t.at[:, cols], sib))
    to_sib.wait()
    pair = 2 * half

    def chip_sum(index, size):
        mine = ptxt[pl.ds(pl.multiple_of(c * side + index * size, size), size)]
        return mine.astype(f32) + sib_in[at(index, size)].astype(f32)

    x_t = []
    for k, p in zip(range(1, NX), xp):
        txo[k - 1] = chip_sum((x + k) % NX, pair).astype(bf16)
        x_t.append(send(txo.at[k - 1], txi.at[k - 1], p))

    for copy in r_z:
        copy.wait()
    total = pimg[at(z, rows)].astype(f32)
    for k in range(NZ - 1):
        total = total + img_in[k].astype(f32)
    img_sum[...] = total.astype(bf16)
    i_m = send(img_sum, img_mate, mate)
    p_z = [
        send(pooled_t.at[:, at(my_zc, 128)], pooled_t.at[:, at(my_zc, 128)], p) for p in zp
    ]
    p_s = [send(pooled_t.at[:, at(my_zc, 128)], pooled_t.at[:, at(my_zc, 128)], sib)]
    loads[2].wait()
    i_m.wait()
    unit_grad = img_sum[...].astype(f32) + img_mate[...].astype(f32)
    img_norm, img_inv = unit_rows(img_ref[...])
    image_grad = unit_back(img_norm, img_inv, unit_grad)
    cotangent = image_grad.astype(bf16)
    cot_t[...] = jnp.transpose(image_grad).astype(bf16)
    own_cot = cot_t[pl.ds(pl.multiple_of(t * eh + my_zc * ec, ec), ec)]
    cot_all[0:ec, at(my_zc, 128)] = own_cot
    for i, n in chunks(width, 256):
        rgrad[:, i : i + n] = (
            contract_last(cotangent, w_proj[i : i + n]) * g2_ref[:, i : i + n]
        )
    rgrad[...] = norm_back(rgrad[...], n_out[...], inv_out)
    resid_cot = rgrad[...].astype(bf16)
    c_sends, g_sends = [], []
    for (kz, kc), p in zip(zc_offsets() + [(0, 0)], zc + [None]):
        slot = ((z + kz) % NZ) * NC + (c + kc) % NC
        cols = at(slot, hid)
        pre_out[:, cols] = (dot(resid_cot, w_down[:, cols]) * slope[:, cols]).astype(bf16)
        if p is None:
            pre_all[at(my_zc, rows)] = pre_out[:, cols]
        else:
            g_sends.append(send(pre_out.at[:, cols], pre_all.at[at(my_zc, rows)], p))
            block = pl.ds(pl.multiple_of(t * eh + slot * ec, ec), ec)
            c_sends.append(
                send(cot_t.at[block], cot_all.at[0:ec, at(my_zc, 128)], p)
            )
    for k, copy in zip(range(1, NZ), p_z):
        copy.wait_recv()
        cols = at(((z + NZ - k) % NZ) * NC + c, 128)
        p_s.append(send(pooled_t.at[:, cols], pooled_t.at[:, cols], sib))
    pre_grad = pre_out[...]
    for i, n in chunks(width, 256):
        mg_out[:, i : i + n] = contract_last(pre_grad, w_up[i : i + n]).astype(bf16)
    g_m = send(mg_out, mg_in, mate)

    for copy in m_s + g_sends:
        copy.wait()
    quarter = width // NX
    wu_x, wp_x = [], []
    for k in [1, 2, 3, 0]:
        b = (x + k) % NX
        wu[b] = dot(mlp_t[at(b, quarter)], pre_all[...]).astype(bf16)
        if k:
            wu_x.append(send(wu.at[b], wui.at[k - 1], xp[k - 1]))
    for copy in c_sends + p_s:
        copy.wait()
    for k in [1, 2, 3, 0]:
        b = (x + k) % NX
        wp[b] = contract_last(pooled_t[at(b, quarter)], cot_all[...]).astype(bf16)
        if k:
            wp_x.append(send(wp.at[b], wpi.at[k - 1], xp[k - 1]))

    for copy in x_t:
        copy.wait()

    def x_total(part):
        mine = ptxt[pl.ds(pl.multiple_of(c * side + (x * NYL + part) * half, half), half)]
        mine = mine.astype(f32) + sib_in[at(x * NYL + part, half)].astype(f32)
        for k in range(NX - 1):
            mine = mine + txi[k, at(part, half)].astype(f32)
        return mine

    tyo[...] = x_total(1 - yl).astype(bf16)
    y_t = send(tyo, tyi, ynb)
    tsum[...] = x_total(yl)
    y_t.wait()
    txt_norm, txt_inv = unit_rows(txt_ref[at(t, half)])
    text_out[at(t, half)] = unit_back(
        txt_norm, txt_inv, tsum[...] + tyi[...].astype(f32)
    ).astype(bf16)
    t_m = same(text_out, t, half, mate)

    g_m.wait()
    dm = (mg_out[...].astype(f32) + mg_in[...].astype(f32)) * g1_ref[...]
    input_out[...] = (rgrad[...] + norm_back(dm, n_in[...], inv_in)).astype(bf16)

    for copy in wu_x + wp_x:
        copy.wait()
    eighth = quarter // 2

    def w_total(own, got, part):
        block = at(part, eighth)
        total = own[x, block].astype(f32)
        for k in range(NX - 1):
            total = total + got[k, block].astype(f32)
        return total

    wyo[:, 0:hid] = w_total(wu, wui, 1 - yl).astype(bf16)
    wyo[:, hid:] = w_total(wp, wpi, 1 - yl).astype(bf16)
    w_y = send(wyo, wyi, ynb)
    wsum[:, 0:hid] = w_total(wu, wui, yl)
    wsum[:, hid:] = w_total(wp, wpi, yl)
    w_y.wait()
    wsum[...] = wsum[...] + wyi[...].astype(f32)
    share = eighth // 8
    for i in range(8):
        wblk_u[i, 0:share] = wsum[share * i : share * (i + 1), 0:hid]
        wblk_p[i, 0:share] = wsum[share * i : share * (i + 1), hid:]
        wblk_u[i, share:] = jnp.zeros((32 - share, hid), f32)
        wblk_p[i, share:] = jnp.zeros((32 - share, 128), f32)
    last = []
    for (kz, kc), p in zip(zc_offsets(), zc):
        slot = ((z + kz) % NZ) * NC + (c + kc) % NC
        last.append(send(wblk_u.at[slot], up_out.at[:, at(my_zc, hid)], p))
        last.append(send(wblk_p.at[slot], proj_out.at[my_zc], p))
    up_out[:, at(my_zc, hid)] = wblk_u[my_zc]
    proj_out[my_zc] = wblk_p[my_zc]
    for copy in m_z + p_z:
        copy.wait_send()
    t_m.wait()
    for copy in last:
        copy.wait()


def local(image_cache, text_cache, labels, layer_input, ln1_gain, ln2_gain, w_up, w_down, proj):
    rows, embed = image_cache.shape
    width = layer_input.shape[1]
    half = rows // 2
    hidden = w_up.shape[1]
    hid = hidden // 8
    ec = embed // 16
    quarter = width // NX
    share = width // 64
    n_sems = 112
    vm = pltpu.VMEM
    scratch = [
        vm(w_up.shape, bf16),
        vm(w_down.shape, bf16),
        vm(proj.shape, bf16),
        vm((NZ * rows, embed), bf16),
        vm((16 * half, embed), bf16),
        vm((NZ, 8, rows), jnp.int32),
        vm((width, 8 * rows), bf16),
        vm((width, 8 * rows), bf16),
        vm((rows, hidden), bf16),
        vm((rows, hidden), f32),
        vm((rows, width), bf16),
        vm((rows, width), bf16),
        vm((rows, width), f32),
        vm((rows, width), f32),
        vm((NZ * rows, 16 * half), f32),
        vm((2, NZ * rows), f32),
        vm((2, 16 * half), f32),
        vm((8, 2, NZ * rows), f32),
        vm((16, 2, 16 * half), f32),
        vm((NZ * rows, 16 * half), bf16),
        vm((16 * half, NZ * rows), bf16),
        vm((NZ * rows, embed), bf16),
        vm((NZ - 1, rows, embed), bf16),
        vm((rows, embed), bf16),
        vm((rows, embed), bf16),
        vm((16 * half, embed), bf16),
        vm((8 * half, embed), bf16),
        vm((NX - 1, 2 * half, embed), bf16),
        vm((NX - 1, 2 * half, embed), bf16),
        vm((half, embed), bf16),
        vm((half, embed), bf16),
        vm((half, embed), f32),
        vm((rows, width), f32),
        vm((embed, rows), bf16),
        vm((128, 8 * rows), bf16),
        vm((rows, hidden), bf16),
        vm((8 * rows, hid), bf16),
        vm((rows, width), bf16),
        vm((rows, width), bf16),
        vm((NX, quarter, 128), bf16),
        vm((NX, quarter, hid), bf16),
        vm((NX - 1, quarter, 128), bf16),
        vm((NX - 1, quarter, hid), bf16),
        vm((quarter // 2, hid + 128), bf16),
        vm((quarter // 2, hid + 128), bf16),
        vm((quarter // 2, hid + 128), f32),
        vm((8, 32, hid), f32),
        vm((8, 32, 128), f32),
        pltpu.SemaphoreType.DMA((n_sems,)),
        pltpu.SemaphoreType.DMA((n_sems,)),
        pltpu.SemaphoreType.DMA((3,)),
    ]
    on_vmem = pl.BlockSpec(memory_space=pltpu.VMEM)
    anywhere = pl.BlockSpec(memory_space=pl.ANY)
    text_grad, input_grad, up, blocks = pl.pallas_call(
        body,
        name="clip_mlp",
        out_shape=[
            jax.ShapeDtypeStruct((rows, embed), bf16),
            jax.ShapeDtypeStruct((rows, width), bf16),
            jax.ShapeDtypeStruct((32, hidden), f32),
            jax.ShapeDtypeStruct((8, 32, 128), f32),
        ],
        in_specs=[on_vmem] * 6 + [anywhere] * 3,
        out_specs=[on_vmem] * 4,
        scratch_shapes=scratch,
        compiler_params=pltpu.CompilerParams(
            collective_id=1, has_side_effects=True, vmem_limit_bytes=VMEM_LIMIT
        ),
    )(
        image_cache,
        text_cache,
        jnp.broadcast_to(labels[None, :], (8, rows)),
        layer_input,
        ln1_gain[None, :],
        ln2_gain[None, :],
        w_up,
        w_down,
        proj,
    )
    up_grad = up[:share]
    proj_grad = blocks[:, :share, :ec].transpose(1, 0, 2).reshape(share, 8 * ec)
    return (text_grad, input_grad, up_grad, proj_grad)


def solution(mesh):
    in_specs = (
        P("dp", None),
        P("dp", None),
        P("dp"),
        P("dp", None),
        P(),
        P(),
        P(None, "tensor"),
        P(None, "tensor"),
        P(),
    )
    out_specs = (P("dp", None), P("dp", None), P("dp", "tensor"), P("dp", "tensor"))
    return jax.shard_map(local, mesh=mesh, in_specs=in_specs, out_specs=out_specs, check_vma=False)
```

time: 1380 us -> 135 us (0.10)
  waiting for transfers between devices: 692 us -> 0 us
  blocking collectives: 575 us -> 0 us
  Pallas kernels: 0 us -> 124 us
  matrix products: 54.5 us -> 0 us
  other arithmetic: 25.7 us -> 0 us
  between operations: 15.5 us -> 0.65 us
    unnamed x6 -> x0, waiting for transfers between devices: 598 us -> none
    unnamed x2 -> x0, blocking collectives: 557 us -> none
    pallas_call x0 -> x1, Pallas kernels: none -> 124 us  [local(): pl.pallas_call(body, name='clip_mlp', out_shape=[jax.ShapeDtypeStruct((ro...]
    psum x2 -> x0, waiting for transfers between devices: 94.1 us -> none  [the longest x1 75 us: local(): img_unit_grad, txt_unit_grad = lax.psum((part_img, part_txt), 'tensor')]
    dot_general x11 -> x0, matrix products: 54.5 us -> none  [the longest x5 27.1 us: contract_last(): lax.dot_general(left, right, (((1,), (1,)), ((), ())), preferred_element_...]
    all_gather x4 -> x0, blocking collectives: 18.4 us -> none  [combined_all(): gathered = jax.tree.map(lambda a: lax.all_gather(a, axis), part)]
  transfers between devices with their start and end apart: 5 -> 0, of which waited for: 3 -> 0; matrix products, arithmetic and copies ran while one was open for 3% -> 0% of each run, Pallas kernels for 0% -> 0%
where the time goes in v2:
time: 135 us
  Pallas kernels  124 us (92%)
  local copies, waits for them, and re-layouts  10.7 us (8%)
    pallas_call x1, Pallas kernels, local(): pl.pallas_call(body, name='clip_mlp', out_shape=[jax.ShapeDtypeStruct((ro...  124 us
    unnamed x3, local copies, waits for them, and re-layouts  5.18 us

profile of v2, /device:TPU:1, one launch (start us, length us, event | category | flops | bytes accessed | tf_op | source)
XLA Modules:
  0.0 135.1 jit_solution(14630181960000693747)
XLA Ops:
  0.6 1.2 broadcast_in_dim.12.lab_ref
  1.9 1.3 broadcast_in_dim.13.g1_ref
  3.2 1.3 broadcast_in_dim.14.g2_ref
  4.5 123.7 %clip_mlp.1 = (bf16[128,1280]{1,0:T(8,128)(2,1)}, bf16[128,1664]{1,0:T(8,128)(2,1)}, f32[32,2048]{1,0:T(8,128)}, f32[8,32,128]{2,1,0:T(8,128)}) custom-call(bf16[128,1280]{1,0:T(8,128)(2,1)} %img_ref.1, bf16[128,1280]{1,0:T(8,128)(2,1)} %txt_ref.1, s32[8,128]{1,0:T(8,128)} %broadcast_in_dim.12.lab_ref, bf16[128,1664]{1,0:T(8,128)(2,1)} %lin_ref.1, ...), custom_call_target="tpu_custom_call" | custom-call | tf_op jit(solution)/shard_map/clip_mlp/pallas_call | solution.py:518
  128.2 0.9 slice_bitcast_fusion
  129.1 0.1 copy.13
  129.2 0.7 reshape.12
  129.9 1.7 %copy.17 = bf16[128,1280]{1,0:T(8,128)(2,1)} copy(bf16[128,1280]{1,0:T(8,128)(2,1)} %get-tuple-element.16) | data formatting | bytes 655360
  131.6 1.8 %copy.18 = bf16[128,1664]{1,0:T(8,128)(2,1)} copy(bf16[128,1664]{1,0:T(8,128)(2,1)} %get-tuple-element.17) | data formatting | bytes 851968
  133.4 1.7 %copy.19 = f32[26,2048]{1,0:T(8,128)} copy(f32[26,2048]{1,0:T(8,128)} %bitcast.3) | data formatting | bytes 425984

commit v3 on v2

--- a/solution.py
+++ b/solution.py
@@ -30,10 +30,10 @@
     def __init__(self, send_sem, recv_sem):
         self.send_sem, self.recv_sem, self.n = send_sem, recv_sem, 0
 
-    def send(self, src, dst, dev):
+    def make(self, src, dst, dev):
         i = self.n
         self.n += 1
-        copy = pltpu.make_async_remote_copy(
+        return pltpu.make_async_remote_copy(
             src_ref=src,
             dst_ref=dst,
             send_sem=self.send_sem.at[i],
@@ -41,6 +41,9 @@
             device_id=dev,
             device_id_type=MESH,
         )
+
+    def send(self, src, dst, dev):
+        copy = self.make(src, dst, dev)
         copy.start()
         return copy
 
@@ -117,19 +120,19 @@
     w_up, w_down, w_proj, img_all, txt_all, lab_all, mlp_t, pooled_t, act, slope,
     res_out, res_in, n_in, n_out, logits, row_st, col_st, rows_all, cols_all,
     grad, grad_t, pimg, img_in, img_sum, img_mate, ptxt, sib_in, txo, txi, tyo, tyi, tsum,
-    rgrad, cot_t, cot_all, pre_out, pre_all, mg_out, mg_in,
-    wp, wu, wpi, wui, wyo, wyi, wsum, wblk_u, wblk_p,
+    rgrad, cot, pre_out, pre_all, mg_out, mg_in,
+    wp, wps, wpo, wpi, wp_sum, wpy, wpyi, wpz, wpzi, wpl, wu, wui, wyo, wyi, wsum, wblk,
     ss, rs, ls,
 ):
     x, yl, z, c, t = coords()
     me = lax.axis_index("dp")
+    gain1, gain2 = g1_ref[...][None, :], g2_ref[...][None, :]
     rows, embed = img_ref.shape
     width = lin_ref.shape[1]
     half = rows // 2
     hidden = up_hbm.shape[1]
     hid = hidden // 8
     eh = embed // 2
-    ec = eh // 8
     sib, mate, ynb = (dp_of(x, yl, z, 1 - c), t), (me, 1 - t), (dp_of(x, 1 - yl, z, c), t)
     zp = [(dp_of(x, yl, (z + k) % NZ, c), t) for k in range(1, NZ)]
     xp = [(dp_of((x + k) % NX, yl, z, c), t) for k in range(1, NX)]
@@ -161,8 +164,7 @@
     img_all[at(z, rows)] = img_unit.astype(bf16)
     txt_unit, _ = unit_rows(txt_ref[at(t, half)])
     txt_all[at(my_slot, half)] = txt_unit.astype(bf16)
-    lab_all[z] = lab_ref[...]
-    cot_all[ec:] = jnp.zeros((128 - ec, 8 * rows), bf16)
+    lab_all[z] = jnp.broadcast_to(lab_ref[...][None, :], (8, rows))
     pl.semaphore_wait(entry, len(greet))
 
     comm = Comm(ss, rs)
@@ -180,18 +182,12 @@
     inputs = lin_ref[...].astype(f32)
     normed_in, inv_in = layer_norm(inputs)
     n_in[...] = normed_in
-    mlp_f = n_in[...] * g1_ref[...]
-    mlp_in = mlp_f.astype(bf16)
+    mlp_in = (n_in[...] * gain1).astype(bf16)
     my_zc = z * NC + c
     for i, n in chunks(width, 128):
         mlp_t[i : i + n, at(my_zc, 128)] = jnp.transpose(
-            n_in[:, i : i + n] * g1_ref[:, i : i + n]
+            n_in[:, i : i + n] * gain1[:, i : i + n]
         ).astype(bf16)
-    t_y.wait_recv()
-    other = c * 8 + x * NYL + (1 - yl)
-    f_x = [same(txt_all, other, half, p) for p in xp]
-    t_s.append(same(txt_all, other, half, sib))
-
     loads[0].wait()
 
     def up_tile(i, _):
@@ -203,6 +199,11 @@
         return _
 
     lax.fori_loop(0, hidden // 256, up_tile, 0)
+    t_y.wait_recv()
+    other = c * 8 + x * NYL + (1 - yl)
+    f_x = [same(txt_all, other, half, p) for p in xp]
+    t_s.append(same(txt_all, other, half, sib))
+
     for k, copy in zip(range(1, NX), t_x):
         copy.wait_recv()
         t_s.append(same(txt_all, c * 8 + ((x + NX - k) % NX) * NYL + yl, half, sib))
@@ -216,9 +217,23 @@
         t_s.append(same(txt_all, c * 8 + ((x + NX - k) % NX) * NYL + (1 - yl), half, sib))
     for copy in i_z + l_z:
         copy.wait()
-    m_z = [
-        send(mlp_t.at[:, at(my_zc, 128)], mlp_t.at[:, at(my_zc, 128)], p) for p in zp
-    ]
+    m_z, m_s = [], []
+
+    def share_mlp(first, size):
+        ref = mlp_t.at[first : first + size, at(my_zc, 128)]
+        m_z.append((first, size, [send(ref, ref, p) for p in zp]))
+        m_s.append(send(ref, ref, sib))
+
+    def pass_mlp():
+        for first, size, copies in m_z:
+            for k, copy in zip(range(1, NZ), copies):
+                copy.wait()
+                ref = mlp_t.at[first : first + size, at(((z + NZ - k) % NZ) * NC + c, 128)]
+                m_s.append(send(ref, ref, sib))
+        m_z.clear()
+
+    cut_a, cut_b = 640, 1152
+    share_mlp(0, cut_a)
     for copy in t_s:
         copy.wait()
     t_y.wait_send()
@@ -259,11 +274,12 @@
     normed_out, inv_out = layer_norm(resid)
     n_out[...] = normed_out
     for i, n in chunks(width, 128):
-        pooled_t[i : i + n, at(my_zc, 128)] = jnp.transpose(
-            n_out[:, i : i + n] * g2_ref[:, i : i + n]
+        pooled_t[i : i + n] = jnp.transpose(
+            n_out[:, i : i + n] * gain2[:, i : i + n]
         ).astype(bf16)
     for copy in stats:
         copy.wait()
+    share_mlp(cut_a, cut_b - cut_a)
 
     row_lse = to_column(merged_lse(rows_all, 8), n_row)
     col_st[0:1] = merged_lse(cols_all, 16)
@@ -305,11 +321,6 @@
     lax.fori_loop(0, embed // 256, txt_tile, 0)
     side = 8 * half
     to_sib = send(ptxt.at[at(1 - c, side)], sib_in, sib)
-    m_s = [send(mlp_t.at[:, at(my_zc, 128)], mlp_t.at[:, at(my_zc, 128)], sib)]
-    for k, copy in zip(range(1, NZ), m_z):
-        copy.wait_recv()
-        cols = at(((z + NZ - k) % NZ) * NC + c, 128)
-        m_s.append(send(mlp_t.at[:, cols], mlp_t.at[:, cols], sib))
     to_sib.wait()
     pair = 2 * half
 
@@ -329,26 +340,35 @@
         total = total + img_in[k].astype(f32)
     img_sum[...] = total.astype(bf16)
     i_m = send(img_sum, img_mate, mate)
-    p_z = [
-        send(pooled_t.at[:, at(my_zc, 128)], pooled_t.at[:, at(my_zc, 128)], p) for p in zp
-    ]
-    p_s = [send(pooled_t.at[:, at(my_zc, 128)], pooled_t.at[:, at(my_zc, 128)], sib)]
+    share_mlp(cut_b, width - cut_b)
     loads[2].wait()
     i_m.wait()
     unit_grad = img_sum[...].astype(f32) + img_mate[...].astype(f32)
     img_norm, img_inv = unit_rows(img_ref[...])
     image_grad = unit_back(img_norm, img_inv, unit_grad)
     cotangent = image_grad.astype(bf16)
-    cot_t[...] = jnp.transpose(image_grad).astype(bf16)
-    own_cot = cot_t[pl.ds(pl.multiple_of(t * eh + my_zc * ec, ec), ec)]
-    cot_all[0:ec, at(my_zc, 128)] = own_cot
+    cot[...] = cotangent
+    eighth = width // 8
+    cot_half = cot[:, at(t, eh)]
+    for q in range(2):
+        for i in range(NX):
+            first = (2 * i + q) * eighth
+            wp[q, i] = dot(pooled_t[first : first + eighth], cot_half).astype(bf16)
+    p_s = send(wp.at[1 - c], wps, sib)
     for i, n in chunks(width, 256):
         rgrad[:, i : i + n] = (
-            contract_last(cotangent, w_proj[i : i + n]) * g2_ref[:, i : i + n]
+            contract_last(cotangent, w_proj[i : i + n]) * gain2[:, i : i + n]
         )
     rgrad[...] = norm_back(rgrad[...], n_out[...], inv_out)
+    pass_mlp()
+    p_s.wait()
+    p_x = []
+    for k, p in zip(range(1, NX), xp):
+        b = (x + k) % NX
+        wpo[k - 1] = (wp[c, b].astype(f32) + wps[b].astype(f32)).astype(bf16)
+        p_x.append(send(wpo.at[k - 1], wpi.at[k - 1], p))
     resid_cot = rgrad[...].astype(bf16)
-    c_sends, g_sends = [], []
+    g_sends = []
     for (kz, kc), p in zip(zc_offsets() + [(0, 0)], zc + [None]):
         slot = ((z + kz) % NZ) * NC + (c + kc) % NC
         cols = at(slot, hid)
@@ -357,14 +377,6 @@
             pre_all[at(my_zc, rows)] = pre_out[:, cols]
         else:
             g_sends.append(send(pre_out.at[:, cols], pre_all.at[at(my_zc, rows)], p))
-            block = pl.ds(pl.multiple_of(t * eh + slot * ec, ec), ec)
-            c_sends.append(
-                send(cot_t.at[block], cot_all.at[0:ec, at(my_zc, 128)], p)
-            )
-    for k, copy in zip(range(1, NZ), p_z):
-        copy.wait_recv()
-        cols = at(((z + NZ - k) % NZ) * NC + c, 128)
-        p_s.append(send(pooled_t.at[:, cols], pooled_t.at[:, cols], sib))
     pre_grad = pre_out[...]
     for i, n in chunks(width, 256):
         mg_out[:, i : i + n] = contract_last(pre_grad, w_up[i : i + n]).astype(bf16)
@@ -372,20 +384,13 @@
 
     for copy in m_s + g_sends:
         copy.wait()
-    quarter = width // NX
-    wu_x, wp_x = [], []
-    for k in [1, 2, 3, 0]:
-        b = (x + k) % NX
-        wu[b] = dot(mlp_t[at(b, quarter)], pre_all[...]).astype(bf16)
-        if k:
-            wu_x.append(send(wu.at[b], wui.at[k - 1], xp[k - 1]))
-    for copy in c_sends + p_s:
-        copy.wait()
-    for k in [1, 2, 3, 0]:
-        b = (x + k) % NX
-        wp[b] = contract_last(pooled_t[at(b, quarter)], cot_all[...]).astype(bf16)
-        if k:
-            wp_x.append(send(wp.at[b], wpi.at[k - 1], xp[k - 1]))
+    wu_x = []
+    for part in (1 - yl, yl):
+        for k in range(NX):
+            b = ((x + k) % NX) * NYL + part
+            wu[b] = dot(mlp_t[at(b, eighth)], pre_all[...]).astype(bf16)
+            if k:
+                wu_x.append(send(wu.at[b], wui.at[len(wu_x)], xp[k - 1]))
 
     for copy in x_t:
         copy.wait()
@@ -408,45 +413,90 @@
     t_m = same(text_out, t, half, mate)
 
     g_m.wait()
-    dm = (mg_out[...].astype(f32) + mg_in[...].astype(f32)) * g1_ref[...]
+    dm = (mg_out[...].astype(f32) + mg_in[...].astype(f32)) * gain1
     input_out[...] = (rgrad[...] + norm_back(dm, n_in[...], inv_in)).astype(bf16)
 
-    for copy in wu_x + wp_x:
-        copy.wait()
-    eighth = quarter // 2
-
-    def w_total(own, got, part):
-        block = at(part, eighth)
-        total = own[x, block].astype(f32)
+    for copy in p_x:
+        copy.wait()
+    total = wp[c, x].astype(f32) + wps[x].astype(f32)
+    for k in range(NX - 1):
+        total = total + wpi[k].astype(f32)
+    wp_sum[...] = total
+    wpy[...] = total.astype(bf16)
+    p_y = comm.make(wpy, wpyi, ynb)
+    p_z = [comm.make(wpz.at[(z + k) % NZ], wpzi.at[k - 1], p) for k, p in zip(range(1, NZ), zp)]
+    p_l = comm.make(wpl.at[1 - c], proj_out, sib)
+
+    @pl.when(c != yl)
+    def _():
+        p_y.start()
+
+    def w_total(first, part):
+        total = wu[x * NYL + part].astype(f32)
         for k in range(NX - 1):
-            total = total + got[k, block].astype(f32)
+            total = total + wui[first + k].astype(f32)
         return total
 
-    wyo[:, 0:hid] = w_total(wu, wui, 1 - yl).astype(bf16)
-    wyo[:, hid:] = w_total(wp, wpi, 1 - yl).astype(bf16)
+    for copy in wu_x[: NX - 1]:
+        copy.wait()
+    wyo[...] = w_total(0, 1 - yl).astype(bf16)
     w_y = send(wyo, wyi, ynb)
-    wsum[:, 0:hid] = w_total(wu, wui, yl)
-    wsum[:, hid:] = w_total(wp, wpi, yl)
+    share = eighth // 8
+
+    @pl.when(c == yl)
+    def _():
+        p_y.wait_recv()
+        wp_sum[...] = wp_sum[...] + wpyi[...].astype(f32)
+        for i in range(NZ):
+            wpz[i, 0 : 2 * share] = wp_sum[2 * share * i : 2 * share * (i + 1)].astype(bf16)
+            wpz[i, 2 * share :] = jnp.zeros((64 - 2 * share, eh), bf16)
+        for copy in p_z:
+            copy.start()
+
+    for copy in wu_x[NX - 1 :]:
+        copy.wait()
+    wsum[...] = w_total(NX - 1, yl)
     w_y.wait()
     wsum[...] = wsum[...] + wyi[...].astype(f32)
-    share = eighth // 8
     for i in range(8):
-        wblk_u[i, 0:share] = wsum[share * i : share * (i + 1), 0:hid]
-        wblk_p[i, 0:share] = wsum[share * i : share * (i + 1), hid:]
-        wblk_u[i, share:] = jnp.zeros((32 - share, hid), f32)
-        wblk_p[i, share:] = jnp.zeros((32 - share, 128), f32)
+        wblk[i, 0:share] = wsum[share * i : share * (i + 1)].astype(bf16)
+        wblk[i, share:] = jnp.zeros((32 - share, hid), bf16)
     last = []
     for (kz, kc), p in zip(zc_offsets(), zc):
         slot = ((z + kz) % NZ) * NC + (c + kc) % NC
-        last.append(send(wblk_u.at[slot], up_out.at[:, at(my_zc, hid)], p))
-        last.append(send(wblk_p.at[slot], proj_out.at[my_zc], p))
-    up_out[:, at(my_zc, hid)] = wblk_u[my_zc]
-    proj_out[my_zc] = wblk_p[my_zc]
-    for copy in m_z + p_z:
-        copy.wait_send()
+        last.append(send(wblk.at[slot], up_out.at[:, at(my_zc, hid)], p))
+    up_out[:, at(my_zc, hid)] = wblk[my_zc]
+
+    @pl.when(c == yl)
+    def _():
+        for copy in p_z:
+            copy.wait()
+        total = wpz[z].astype(f32)
+        for k in range(NZ - 1):
+            total = total + wpzi[k].astype(f32)
+        wp_sum[0:64] = total
+        for i in range(NC):
+            wpl[i, 0:share] = wp_sum[share * i : share * (i + 1)]
+            wpl[i, share:] = jnp.zeros((32 - share, eh), f32)
+        p_l.start()
+        proj_out[...] = wpl[c]
+        p_l.wait_send()
+
+    @pl.when(c != yl)
+    def _():
+        p_y.wait_send()
+        p_l.wait_recv()
+
     t_m.wait()
     for copy in last:
         copy.wait()
+
+
+def finish(text_ref, input_ref, up_ref, proj_ref, text_out, input_out, up_out, proj_out):
+    text_out[...] = text_ref[...]
+    input_out[...] = input_ref[...]
+    up_out[...] = up_ref[0 : up_out.shape[0]].astype(f32)
+    proj_out[...] = proj_ref[0 : proj_out.shape[0]]
 
 
 def local(image_cache, text_cache, labels, layer_input, ln1_gain, ln2_gain, w_up, w_down, proj):
@@ -455,10 +505,10 @@
     half = rows // 2
     hidden = w_up.shape[1]
     hid = hidden // 8
-    ec = embed // 16
-    quarter = width // NX
+    eh = embed // 2
+    eighth = width // 8
     share = width // 64
-    n_sems = 112
+    n_sems = 128
     vm = pltpu.VMEM
     scratch = [
         vm(w_up.shape, bf16),
@@ -468,7 +518,7 @@
         vm((16 * half, embed), bf16),
         vm((NZ, 8, rows), jnp.int32),
         vm((width, 8 * rows), bf16),
-        vm((width, 8 * rows), bf16),
+        vm((width, rows), bf16),
         vm((rows, hidden), bf16),
         vm((rows, hidden), f32),
         vm((rows, width), bf16),
@@ -494,35 +544,41 @@
         vm((half, embed), bf16),
         vm((half, embed), f32),
         vm((rows, width), f32),
-        vm((embed, rows), bf16),
-        vm((128, 8 * rows), bf16),
+        vm((rows, embed), bf16),
         vm((rows, hidden), bf16),
         vm((8 * rows, hid), bf16),
         vm((rows, width), bf16),
         vm((rows, width), bf16),
-        vm((NX, quarter, 128), bf16),
-        vm((NX, quarter, hid), bf16),
-        vm((NX - 1, quarter, 128), bf16),
-        vm((NX - 1, quarter, hid), bf16),
-        vm((quarter // 2, hid + 128), bf16),
-        vm((quarter // 2, hid + 128), bf16),
-        vm((quarter // 2, hid + 128), f32),
-        vm((8, 32, hid), f32),
-        vm((8, 32, 128), f32),
+        vm((NYL, NX, eighth, eh), bf16),
+        vm((NX, eighth, eh), bf16),
+        vm((NX - 1, eighth, eh), bf16),
+        vm((NX - 1, eighth, eh), bf16),
+        vm((eighth, eh), f32),
+        vm((eighth, eh), bf16),
+        vm((eighth, eh), bf16),
+        vm((NZ, 64, eh), bf16),
+        vm((NZ - 1, 64, eh), bf16),
+        vm((NC, 32, eh), f32),
+        vm((8, eighth, hid), bf16),
+        vm((2 * NX - 2, eighth, hid), bf16),
+        vm((eighth, hid), bf16),
+        vm((eighth, hid), bf16),
+        vm((eighth, hid), f32),
+        vm((8, 32, hid), bf16),
         pltpu.SemaphoreType.DMA((n_sems,)),
         pltpu.SemaphoreType.DMA((n_sems,)),
         pltpu.SemaphoreType.DMA((3,)),
     ]
     on_vmem = pl.BlockSpec(memory_space=pltpu.VMEM)
     anywhere = pl.BlockSpec(memory_space=pl.ANY)
-    text_grad, input_grad, up, blocks = pl.pallas_call(
+    parts = pl.pallas_call(
         body,
         name="clip_mlp",
         out_shape=[
             jax.ShapeDtypeStruct((rows, embed), bf16),
             jax.ShapeDtypeStruct((rows, width), bf16),
-            jax.ShapeDtypeStruct((32, hidden), f32),
-            jax.ShapeDtypeStruct((8, 32, 128), f32),
+            jax.ShapeDtypeStruct((32, hidden), bf16),
+            jax.ShapeDtypeStruct((32, eh), f32),
         ],
         in_specs=[on_vmem] * 6 + [anywhere] * 3,
         out_specs=[on_vmem] * 4,
@@ -533,17 +589,26 @@
     )(
         image_cache,
         text_cache,
-        jnp.broadcast_to(labels[None, :], (8, rows)),
+        labels,
         layer_input,
-        ln1_gain[None, :],
-        ln2_gain[None, :],
+        ln1_gain,
+        ln2_gain,
         w_up,
         w_down,
         proj,
     )
-    up_grad = up[:share]
-    proj_grad = blocks[:, :share, :ec].transpose(1, 0, 2).reshape(share, 8 * ec)
-    return (text_grad, input_grad, up_grad, proj_grad)
+    return pl.pallas_call(
+        finish,
+        name="finish",
+        out_shape=[
+            jax.ShapeDtypeStruct((rows, embed), bf16),
+            jax.ShapeDtypeStruct((rows, width), bf16),
+            jax.ShapeDtypeStruct((share, hidden), f32),
+            jax.ShapeDtypeStruct((share, eh), f32),
+        ],
+        in_specs=[on_vmem] * 4,
+        out_specs=[on_vmem] * 4,
+    )(*parts)
 
 
 def solution(mesh):

time: 135 us -> 115 us (0.85)
  local copies, waits for them, and re-layouts: 10.7 us -> 0 us
  Pallas kernels: 124 us -> 114 us
    pallas_call x1, Pallas kernels: 124 us -> 112 us  [local(): pl.pallas_call(body, name='clip_mlp', out_shape=[jax.ShapeDtypeStruct((ro...]
    unnamed x3 -> x0, local copies, waits for them, and re-layouts: 5.18 us -> none
    broadcast_in_dim x3 -> x0, local copies, waits for them, and re-layouts: 3.84 us -> none  [the longest x1 1.29 us: local(): ln1_gain[None, :]]
    pallas_call x0 -> x1, Pallas kernels: none -> 2.16 us  [local(): pl.pallas_call(finish, name='finish', out_shape=[jax.ShapeDtypeStruct((ro...]
where the time goes in v3:
time: 115 us; the launch traced here: 114 us
  Pallas kernels  114 us (99%)
    pallas_call x1, Pallas kernels, local(): pl.pallas_call(body, name='clip_mlp', out_shape=[jax.ShapeDtypeStruct((ro...  112 us

profile of v3, /device:TPU:1, one launch (start us, length us, event | category | flops | bytes accessed | tf_op | source)
XLA Modules:
  0.0 114.4 jit_solution(250262065770629381)
XLA Ops:
  0.6 111.6 %clip_mlp.1 = (bf16[128,1280]{1,0:T(8,128)(2,1)}, bf16[128,1664]{1,0:T(8,128)(2,1)}, bf16[32,2048]{1,0:T(8,128)(2,1)}, f32[32,640]{1,0:T(8,128)}) custom-call(bf16[128,1280]{1,0:T(8,128)(2,1)} %img_ref.1, bf16[128,1280]{1,0:T(8,128)(2,1)} %txt_ref.1, s32[128]{0:T(128)} %lab_ref.1, bf16[128,1664]{1,0:T(8,128)(2,1)} %lin_ref.1, f32[1664]{0:T(1024)} %g1_ref.1, ...), custom_call_target="tpu_custom_call" | custom-call | tf_op jit(solution)/shard_map/clip_mlp/pallas_call | solution.py:574
  112.3 2.2 %finish.1 = (bf16[128,1280]{1,0:T(8,128)(2,1)}, bf16[128,1664]{1,0:T(8,128)(2,1)}, f32[26,2048]{1,0:T(8,128)}, f32[26,640]{1,0:T(8,128)}) custom-call(bf16[128,1280]{1,0:T(8,128)(2,1)} %get-tuple-element.8.text_ref, bf16[128,1664]{1,0:T(8,128)(2,1)} %get-tuple-element.9.input_ref, bf16[32,2048]{1,0:T(8,128)(2,1)} %get-tuple-element.10.up_ref, ...), custom_call_target="tpu_custom_call" | custom-call | tf_op jit(solution)/shard_map/finish/pallas_call | solution.py:600

commit v4 on v3

--- a/solution.py
+++ b/solution.py
@@ -24,6 +24,42 @@
     yl = (d // (NC * NZ)) % NYL
     x = d // (NC * NZ * NYL)
     return x, yl, z, c, lax.axis_index("tensor")
+
+
+class Ring:
+    def __init__(self, send, ref, size, slot, pos, peers):
+        self.send, self.ref, self.size, self.slot, self.pos = send, ref, size, slot, pos
+        self.right, self.left = peers[0], peers[2]
+        self.right_top = self.push(0, 0, self.right)
+        self.left_low = self.push(0, 1, self.left)
+        self.right_low = self.push(0, 1, self.right)
+        self.left_top = self.push(0, 0, self.left)
+
+    def push(self, offset, part, dev):
+        n = self.size // 2
+        first = pl.multiple_of(self.slot((self.pos + offset) % 4) * self.size + part * n, n)
+        ref = self.ref.at[pl.ds(first, n)]
+        return self.send(ref, ref, dev)
+
+    def forward(self):
+        self.right_top.wait_recv()
+        self.right_far = self.push(3, 0, self.right)
+        self.left_low.wait_recv()
+        self.left_far = self.push(1, 1, self.left)
+
+    def near(self):
+        self.right_low.wait_recv()
+        self.left_top.wait_recv()
+
+    def far(self):
+        self.right_far.wait_recv()
+        self.left_far.wait_recv()
+
+    def drain(self):
+        for copy in (self.right_top, self.left_low, self.right_low, self.left_top):
+            copy.wait_send()
+        self.right_far.wait_send()
+        self.left_far.wait_send()
 
 
 class Comm:
@@ -115,18 +151,18 @@
 
 
 def body(
-    img_ref, txt_ref, lab_ref, lin_ref, g1_ref, g2_ref, up_hbm, down_hbm, proj_hbm,
-    text_out, input_out, up_out, proj_out,
+    img_hbm, txt_hbm, lab_hbm, lin_hbm, g1_hbm, g2_hbm, up_hbm, down_hbm, proj_hbm,
+    text_hbm, input_hbm, up_grad_hbm, proj_grad_hbm,
+    img_ref, txt_ref, lab_ref, lin_ref, g1_ref, g2_ref, text_out, input_out, up_out, proj_out,
     w_up, w_down, w_proj, img_all, txt_all, lab_all, mlp_t, pooled_t, act, slope,
     res_out, res_in, n_in, n_out, logits, row_st, col_st, rows_all, cols_all,
-    grad, grad_t, pimg, img_in, img_sum, img_mate, ptxt, sib_in, txo, txi, tyo, tyi, tsum,
+    grad, grad_t, pimg, r_first, r_near, r_sum, r_last, img_sum, img_mate, ptxt, sib_in, txo, txi, tyo, tyi, tsum,
     rgrad, cot, pre_out, pre_all, mg_out, mg_in,
     wp, wps, wpo, wpi, wp_sum, wpy, wpyi, wpz, wpzi, wpl, wu, wui, wyo, wyi, wsum, wblk,
     ss, rs, ls,
 ):
     x, yl, z, c, t = coords()
     me = lax.axis_index("dp")
-    gain1, gain2 = g1_ref[...][None, :], g2_ref[...][None, :]
     rows, embed = img_ref.shape
     width = lin_ref.shape[1]
     half = rows // 2
@@ -150,15 +186,31 @@
     cross = [p for (kz, kc), p in zip(zc_offsets(), zc) if kz and kc]
     greet = row_peers + col_peers + cross
     entry = pltpu.get_barrier_semaphore()
+    small = [
+        pltpu.make_async_copy(src, dst, ls.at[i])
+        for i, (src, dst) in enumerate(
+            [
+                (img_hbm, img_ref),
+                (txt_hbm, txt_ref),
+                (lab_hbm, lab_ref),
+                (lin_hbm, lin_ref),
+                (g1_hbm, g1_ref),
+                (g2_hbm, g2_ref),
+            ]
+        )
+    ]
+    loads = [
+        pltpu.make_async_copy(up_hbm, w_up, ls.at[6]),
+        pltpu.make_async_copy(down_hbm, w_down, ls.at[7]),
+        pltpu.make_async_copy(proj_hbm, w_proj, ls.at[8]),
+    ]
+    for copy in small + loads:
+        copy.start()
     for peer in greet:
         pl.semaphore_signal(entry, inc=1, device_id=peer, device_id_type=MESH)
-    loads = [
-        pltpu.make_async_copy(up_hbm, w_up, ls.at[0]),
-        pltpu.make_async_copy(down_hbm, w_down, ls.at[1]),
-        pltpu.make_async_copy(proj_hbm, w_proj, ls.at[2]),
-    ]
-    for copy in loads:
-        copy.start()
+    for copy in small:
+        copy.wait()
+    gain1, gain2 = g1_ref[...][None, :], g2_ref[...][None, :]
     my_slot = c * 8 + x * NYL + yl
     img_unit, _ = unit_rows(img_ref[...])
     img_all[at(z, rows)] = img_unit.astype(bf16)
@@ -174,8 +226,12 @@
         return send(ref.at[at(index, size)], ref.at[at(index, size)], dev)
 
     t_y = same(txt_all, my_slot, half, ynb)
-    t_x = [same(txt_all, my_slot, half, p) for p in xp]
-    i_z = [same(img_all, z, rows, p) for p in zp]
+
+    def txt_slot(part):
+        return lambda pos: c * 8 + pos * NYL + part
+
+    t_x = Ring(send, txt_all, half, txt_slot(yl), x, xp)
+    i_z = Ring(send, img_all, rows, lambda pos: pos, z, zp)
     l_z = [send(lab_all.at[z], lab_all.at[z], p) for p in zp]
     t_s = [same(txt_all, my_slot, half, sib)]
 
@@ -199,24 +255,32 @@
         return _
 
     lax.fori_loop(0, hidden // 256, up_tile, 0)
+    def to_sibling(part, offsets):
+        for k in offsets:
+            t_s.append(same(txt_all, txt_slot(part)((x + k) % NX), half, sib))
+
+    t_x.forward()
     t_y.wait_recv()
-    other = c * 8 + x * NYL + (1 - yl)
-    f_x = [same(txt_all, other, half, p) for p in xp]
-    t_s.append(same(txt_all, other, half, sib))
-
-    for k, copy in zip(range(1, NX), t_x):
-        copy.wait_recv()
-        t_s.append(same(txt_all, c * 8 + ((x + NX - k) % NX) * NYL + yl, half, sib))
+    f_x = Ring(send, txt_all, half, txt_slot(1 - yl), x, xp)
+    to_sibling(1 - yl, [0])
+    i_z.forward()
     loads[1].wait()
     acts = act[...]
     for i, n in chunks(width, 256):
+        if i == 768:
+            f_x.forward()
         res_out[:, i : i + n] = contract_last(acts, w_down[i : i + n]).astype(bf16)
     res_c = send(res_out, res_in, mate)
-    for k, copy in zip(range(1, NX), f_x):
-        copy.wait_recv()
-        t_s.append(same(txt_all, c * 8 + ((x + NX - k) % NX) * NYL + (1 - yl), half, sib))
-    for copy in i_z + l_z:
-        copy.wait()
+    t_x.near()
+    to_sibling(yl, [1, 3])
+    t_x.far()
+    to_sibling(yl, [2])
+    f_x.near()
+    to_sibling(1 - yl, [1, 3])
+    i_z.near()
+    f_x.far()
+    to_sibling(1 - yl, [2])
+    i_z.far()
     m_z, m_s = [], []
 
     def share_mlp(first, size):
@@ -232,13 +296,13 @@
                 m_s.append(send(ref, ref, sib))
         m_z.clear()
 
-    cut_a, cut_b = 640, 1152
+    cut_a, cut_b = 512, 768
     share_mlp(0, cut_a)
-    for copy in t_s:
+    for copy in t_s + l_z:
         copy.wait()
     t_y.wait_send()
-    for copy in t_x + f_x:
-        copy.wait_send()
+    for ring in (t_x, f_x, i_z):
+        ring.drain()
 
     n_row, n_col = img_all.shape[0], txt_all.shape[0]
     tile = 256
@@ -302,16 +366,21 @@
 
     lax.fori_loop(0, n_col // tile, grad_tile, 0)
 
-    def img_tile(i, _):
-        cols = at(i, 256)
+    right, left = zp[0], zp[2]
+    z_right, z_left, z_far = (z + 1) % NZ, (z + 3) % NZ, (z + 2) % NZ
+
+    def strip(pos, part, cols):
+        return pl.ds(pl.multiple_of(pos * rows + part * half, half), half), cols
+
+    parts = [slice(i, i + 256) for i in range(0, embed, 256)]
+    first_r, first_l, near_r, near_l = [], [], [], []
+    for cols in parts:
         pimg[:, cols] = (logit_scale * dot(grad[...], txt_all[:, cols])).astype(bf16)
-        return _
-
-    lax.fori_loop(0, embed // 256, img_tile, 0)
-    r_z = [
-        send(pimg.at[at((z + k) % NZ, rows)], img_in.at[k - 1], p)
-        for k, p in zip(range(1, NZ), zp)
-    ]
+        first_r.append(send(pimg.at[strip(z_far, 0, cols)], r_first.at[0, :, cols], right))
+        first_l.append(send(pimg.at[strip(z_far, 1, cols)], r_first.at[1, :, cols], left))
+    for cols in parts:
+        near_r.append(send(pimg.at[strip(z_right, 1, cols)], r_near.at[0, :, cols], right))
+        near_l.append(send(pimg.at[strip(z_left, 0, cols)], r_near.at[1, :, cols], left))
 
     def txt_tile(i, _):
         cols = at(i, 256)
@@ -321,6 +390,19 @@
     lax.fori_loop(0, embed // 256, txt_tile, 0)
     side = 8 * half
     to_sib = send(ptxt.at[at(1 - c, side)], sib_in, sib)
+    sum_r, sum_l = [], []
+    for cols, copy_r, copy_l in zip(parts, first_r, first_l):
+        copy_r.wait()
+        r_sum[0, :, cols] = (
+            pimg[strip(z_right, 0, cols)].astype(f32) + r_first[0, :, cols].astype(f32)
+        ).astype(bf16)
+        sum_r.append(send(r_sum.at[0, :, cols], r_last.at[0, :, cols], right))
+        copy_l.wait()
+        r_sum[1, :, cols] = (
+            pimg[strip(z_left, 1, cols)].astype(f32) + r_first[1, :, cols].astype(f32)
+        ).astype(bf16)
+        sum_l.append(send(r_sum.at[1, :, cols], r_last.at[1, :, cols], left))
+    share_mlp(cut_b, width - cut_b)
     to_sib.wait()
     pair = 2 * half
 
@@ -333,16 +415,26 @@
         txo[k - 1] = chip_sum((x + k) % NX, pair).astype(bf16)
         x_t.append(send(txo.at[k - 1], txi.at[k - 1], p))
 
-    for copy in r_z:
-        copy.wait()
-    total = pimg[at(z, rows)].astype(f32)
-    for k in range(NZ - 1):
-        total = total + img_in[k].astype(f32)
-    img_sum[...] = total.astype(bf16)
-    i_m = send(img_sum, img_mate, mate)
-    share_mlp(cut_b, width - cut_b)
+    i_m = []
+    for i, cols in enumerate(parts):
+        near_l[i].wait()
+        sum_r[i].wait()
+        img_sum[0:half, cols] = (
+            pimg[strip(z, 0, cols)].astype(f32)
+            + r_last[0, :, cols].astype(f32)
+            + r_near[1, :, cols].astype(f32)
+        ).astype(bf16)
+        near_r[i].wait()
+        sum_l[i].wait()
+        img_sum[half:, cols] = (
+            pimg[strip(z, 1, cols)].astype(f32)
+            + r_last[1, :, cols].astype(f32)
+            + r_near[0, :, cols].astype(f32)
+        ).astype(bf16)
+        i_m.append(send(img_sum.at[:, cols], img_mate.at[:, cols], mate))
     loads[2].wait()
-    i_m.wait()
+    for copy in i_m:
+        copy.wait()
     unit_grad = img_sum[...].astype(f32) + img_mate[...].astype(f32)
     img_norm, img_inv = unit_rows(img_ref[...])
     image_grad = unit_back(img_norm, img_inv, unit_grad)
@@ -360,16 +452,16 @@
             contract_last(cotangent, w_proj[i : i + n]) * gain2[:, i : i + n]
         )
     rgrad[...] = norm_back(rgrad[...], n_out[...], inv_out)
-    pass_mlp()
-    p_s.wait()
-    p_x = []
-    for k, p in zip(range(1, NX), xp):
-        b = (x + k) % NX
-        wpo[k - 1] = (wp[c, b].astype(f32) + wps[b].astype(f32)).astype(bf16)
-        p_x.append(send(wpo.at[k - 1], wpi.at[k - 1], p))
     resid_cot = rgrad[...].astype(bf16)
     g_sends = []
-    for (kz, kc), p in zip(zc_offsets() + [(0, 0)], zc + [None]):
+    p_x = []
+    for i, ((kz, kc), p) in enumerate(zip(zc_offsets() + [(0, 0)], zc + [None])):
+        if i == 3:
+            p_s.wait()
+            for k, peer in zip(range(1, NX), xp):
+                b = (x + k) % NX
+                wpo[k - 1] = (wp[c, b].astype(f32) + wps[b].astype(f32)).astype(bf16)
+                p_x.append(send(wpo.at[k - 1], wpi.at[k - 1], peer))
         slot = ((z + kz) % NZ) * NC + (c + kc) % NC
         cols = at(slot, hid)
         pre_out[:, cols] = (dot(resid_cot, w_down[:, cols]) * slope[:, cols]).astype(bf16)
@@ -377,11 +469,30 @@
             pre_all[at(my_zc, rows)] = pre_out[:, cols]
         else:
             g_sends.append(send(pre_out.at[:, cols], pre_all.at[at(my_zc, rows)], p))
+    for copy in x_t:
+        copy.wait()
+
+    def x_total(part):
+        mine = ptxt[pl.ds(pl.multiple_of(c * side + (x * NYL + part) * half, half), half)]
+        mine = mine.astype(f32) + sib_in[at(x * NYL + part, half)].astype(f32)
+        for k in range(NX - 1):
+            mine = mine + txi[k, at(part, half)].astype(f32)
+        return mine
+
+    tyo[...] = x_total(1 - yl).astype(bf16)
+    y_t = send(tyo, tyi, ynb)
+    tsum[...] = x_total(yl)
     pre_grad = pre_out[...]
     for i, n in chunks(width, 256):
         mg_out[:, i : i + n] = contract_last(pre_grad, w_up[i : i + n]).astype(bf16)
     g_m = send(mg_out, mg_in, mate)
 
+    pass_mlp()
+    y_t.wait()
+    txt_norm, txt_inv = unit_rows(txt_ref[at(t, half)])
+    text_out[at(t, half)] = unit_back(
+        txt_norm, txt_inv, tsum[...] + tyi[...].astype(f32)
+    ).astype(bf16)
     for copy in m_s + g_sends:
         copy.wait()
     wu_x = []
@@ -391,30 +502,6 @@
             wu[b] = dot(mlp_t[at(b, eighth)], pre_all[...]).astype(bf16)
             if k:
                 wu_x.append(send(wu.at[b], wui.at[len(wu_x)], xp[k - 1]))
-
-    for copy in x_t:
-        copy.wait()
-
-    def x_total(part):
-        mine = ptxt[pl.ds(pl.multiple_of(c * side + (x * NYL + part) * half, half), half)]
-        mine = mine.astype(f32) + sib_in[at(x * NYL + part, half)].astype(f32)
-        for k in range(NX - 1):
-            mine = mine + txi[k, at(part, half)].astype(f32)
-        return mine
-
-    tyo[...] = x_total(1 - yl).astype(bf16)
-    y_t = send(tyo, tyi, ynb)
-    tsum[...] = x_total(yl)
-    y_t.wait()
-    txt_norm, txt_inv = unit_rows(txt_ref[at(t, half)])
-    text_out[at(t, half)] = unit_back(
-        txt_norm, txt_inv, tsum[...] + tyi[...].astype(f32)
-    ).astype(bf16)
-    t_m = same(text_out, t, half, mate)
-
-    g_m.wait()
-    dm = (mg_out[...].astype(f32) + mg_in[...].astype(f32)) * gain1
-    input_out[...] = (rgrad[...] + norm_back(dm, n_in[...], inv_in)).astype(bf16)
 
     for copy in p_x:
         copy.wait()
@@ -431,6 +518,22 @@
     def _():
         p_y.start()
 
+    g_m.wait()
+    dm = (mg_out[...].astype(f32) + mg_in[...].astype(f32)) * gain1
+    input_out[...] = (rgrad[...] + norm_back(dm, n_in[...], inv_in)).astype(bf16)
+    stores = [
+        pltpu.make_async_copy(src, dst, ls.at[9 + i])
+        for i, (src, dst) in enumerate(
+            [
+                (input_out, input_hbm),
+                (text_out, text_hbm),
+                (up_out, up_grad_hbm),
+                (proj_out, proj_grad_hbm),
+            ]
+        )
+    ]
+    stores[0].start()
+
     def w_total(first, part):
         total = wu[x * NYL + part].astype(f32)
         for k in range(NX - 1):
@@ -441,6 +544,7 @@
         copy.wait()
     wyo[...] = w_total(0, 1 - yl).astype(bf16)
     w_y = send(wyo, wyi, ynb)
+    t_m = same(text_out, t, half, mate)
     share = eighth // 8
 
     @pl.when(c == yl)
@@ -487,8 +591,13 @@
         p_y.wait_send()
         p_l.wait_recv()
 
+    stores[3].start()
     t_m.wait()
+    stores[1].start()
     for copy in last:
+        copy.wait()
+    stores[2].start()
+    for copy in stores:
         copy.wait()
 
 
@@ -508,9 +617,19 @@
     eh = embed // 2
     eighth = width // 8
     share = width // 64
-    n_sems = 128
+    n_sems = 192
     vm = pltpu.VMEM
     scratch = [
+        vm((rows, embed), bf16),
+        vm((rows, embed), bf16),
+        vm((rows,), jnp.int32),
+        vm((rows, width), bf16),
+        vm((width,), f32),
+        vm((width,), f32),
+        vm((rows, embed), bf16),
+        vm((rows, width), bf16),
+        vm((32, hidden), bf16),
+        vm((32, eh), f32),
         vm(w_up.shape, bf16),
         vm(w_down.shape, bf16),
         vm(proj.shape, bf16),
@@ -533,7 +652,10 @@
         vm((NZ * rows, 16 * half), bf16),
         vm((16 * half, NZ * rows), bf16),
         vm((NZ * rows, embed), bf16),
-        vm((NZ - 1, rows, embed), bf16),
+        vm((2, half, embed), bf16),
+        vm((2, half, embed), bf16),
+        vm((2, half, embed), bf16),
+        vm((2, half, embed), bf16),
         vm((rows, embed), bf16),
         vm((rows, embed), bf16),
         vm((16 * half, embed), bf16),
@@ -567,7 +689,7 @@
         vm((8, 32, hid), bf16),
         pltpu.SemaphoreType.DMA((n_sems,)),
         pltpu.SemaphoreType.DMA((n_sems,)),
-        pltpu.SemaphoreType.DMA((3,)),
+        pltpu.SemaphoreType.DMA((13,)),
     ]
     on_vmem = pl.BlockSpec(memory_space=pltpu.VMEM)
     anywhere = pl.BlockSpec(memory_space=pl.ANY)
@@ -580,8 +702,8 @@
             jax.ShapeDtypeStruct((32, hidden), bf16),
             jax.ShapeDtypeStruct((32, eh), f32),
         ],
-        in_specs=[on_vmem] * 6 + [anywhere] * 3,
-        out_specs=[on_vmem] * 4,
+        in_specs=[anywhere] * 9,
+        out_specs=[anywhere] * 4,
         scratch_shapes=scratch,
         compiler_params=pltpu.CompilerParams(
             collective_id=1, has_side_effects=True, vmem_limit_bytes=VMEM_LIMIT

time: 115 us -> 97.8 us (0.85)
  the two profiles are of different devices: /device:TPU:1 before, /device:TPU:17 now
where the time goes in v4:
time: 97.8 us; the launch traced here: 97.7 us
  Pallas kernels  97 us (99%)
    pallas_call x1, Pallas kernels, local(): pl.pallas_call(body, name='clip_mlp', out_shape=[jax.ShapeDtypeStruct((ro...  94.9 us
    pallas_call x1, Pallas kernels, local(): pl.pallas_call(finish, name='finish', out_shape=[jax.ShapeDtypeStruct((ro...  2.16 us

profile of v4, /device:TPU:17, one launch (start us, length us, event | category | flops | bytes accessed | tf_op | source)
XLA Modules:
  0.0 97.7 jit_solution(9057091453297833534)
XLA Ops:
  0.6 94.9 %clip_mlp.1 = (bf16[128,1280]{1,0:T(8,128)(2,1)}, bf16[128,1664]{1,0:T(8,128)(2,1)}, bf16[32,2048]{1,0:T(8,128)(2,1)}, f32[32,640]{1,0:T(8,128)}) custom-call(bf16[128,1280]{1,0:T(8,128)(2,1)} %img_hbm.1, bf16[128,1280]{1,0:T(8,128)(2,1)} %txt_hbm.1, s32[128]{0:T(128)} %lab_hbm.1, bf16[128,1664]{1,0:T(8,128)(2,1)} %lin_hbm.1, f32[1664]{0:T(1024)} %g1_hbm.1, ...), custom_call_target="tpu_custom_call" | custom-call | tf_op jit(solution)/shard_map/clip_mlp/pallas_call | solution.py:696
  95.5 2.2 %finish.1 = (bf16[128,1280]{1,0:T(8,128)(2,1)}, bf16[128,1664]{1,0:T(8,128)(2,1)}, f32[26,2048]{1,0:T(8,128)}, f32[26,640]{1,0:T(8,128)}) custom-call(bf16[128,1280]{1,0:T(8,128)(2,1)} %get-tuple-element.8.text_ref, bf16[128,1664]{1,0:T(8,128)(2,1)} %get-tuple-element.9.input_ref, bf16[32,2048]{1,0:T(8,128)(2,1)} %get-tuple-element.10.up_ref, ...), custom_call_target="tpu_custom_call" | custom-call | tf_op jit(solution)/shard_map/finish/pallas_call | solution.py:722

commit v5 on v4

v5 whole, which is shorter than its diff:
```python
import jax
import jax.numpy as jnp
from jax import lax
from jax.experimental import pallas as pl
from jax.experimental.pallas import tpu as pltpu
from jax.sharding import PartitionSpec as P

logit_scale = 100.0
MESH = pl.DeviceIdType.MESH
NX, NYL, NZ, NC = 4, 2, 4, 2
bf16 = jnp.bfloat16
f32 = jnp.float32
VMEM_LIMIT = 60 * 1024 * 1024


def dp_of(x, yl, z, c):
    return ((x * NYL + yl) * NZ + z) * NC + c


def coords():
    d = lax.axis_index("dp")
    c = d % NC
    z = (d // NC) % NZ
    yl = (d // (NC * NZ)) % NYL
    x = d // (NC * NZ * NYL)
    return x, yl, z, c, lax.axis_index("tensor")


class Comm:
    def __init__(self, sems):
        self.sems, self.n = sems, 0

    def new(self):
        self.n += 1
        return self.sems.at[self.n - 1]

    def make(self, src, dst, dev, sent=None, got=None):
        return pltpu.make_async_remote_copy(
            src_ref=src,
            dst_ref=dst,
            send_sem=self.new() if sent is None else sent,
            recv_sem=self.new() if got is None else got,
            device_id=dev,
            device_id_type=MESH,
        )

    def send(self, src, dst, dev, sent=None, got=None):
        copy = self.make(src, dst, dev, sent, got)
        copy.start()
        return copy


def wait_all(sem, ref):
    pltpu.make_async_copy(ref, ref, sem).wait()


class Ring:
    def __init__(self, comm, ref, size, slot, pos, peers, sent):
        self.comm, self.ref, self.size, self.slot, self.pos = comm, ref, size, slot, pos
        self.right, self.left, self.sent = peers[0], peers[2], sent
        self.got_near, self.got_far = comm.new(), comm.new()
        self.right_top = self.push(0, 0, self.right)
        self.left_low = self.push(0, 1, self.left)
        self.push(0, 1, self.right, self.got_near)
        self.push(0, 0, self.left, self.got_near)

    def push(self, offset, part, dev, got=None):
        n = self.size // 2
        first = pl.multiple_of(self.slot((self.pos + offset) % 4) * self.size + part * n, n)
        ref = self.ref.at[pl.ds(first, n)]
        return self.comm.send(ref, ref, dev, self.sent, got)

    def forward(self):
        self.right_top.wait_recv()
        self.push(3, 0, self.right, self.got_far)
        self.left_low.wait_recv()
        self.push(1, 1, self.left, self.got_far)

    def near(self):
        wait_all(self.got_near, self.ref.at[0 : self.size])

    def far(self):
        wait_all(self.got_far, self.ref.at[0 : self.size])


class RingSum:
    def __init__(self, comm, top, low, held, pos, peers, sent, two_blocks):
        self.comm, self.top, self.low, self.held, self.pos = comm, top, low, held, pos
        self.right, self.left, self.sent = peers[0], peers[2], sent
        self.two_blocks, self.got = two_blocks, comm.new()

    def at(self, offset):
        pos = (self.pos + offset) % 4
        return self.top(pos), self.low(pos)

    def first(self):
        top, low = self.at(2)
        self.first_r = self.comm.send(top, self.held(0, 0), self.right, self.sent)
        self.first_l = self.comm.send(low, self.held(0, 1), self.left, self.sent)

    def near(self):
        self.comm.send(self.at(1)[1], self.held(1, 1), self.right, self.sent, self.got)
        self.comm.send(self.at(3)[0], self.held(1, 0), self.left, self.sent, self.got)

    def pass_on(self):
        self.first_r.wait_recv()
        added = self.at(1)[0][...].astype(f32) + self.held(0, 0)[...].astype(f32)
        self.held(2, 0)[...] = added.astype(bf16)
        self.comm.send(self.held(2, 0), self.held(3, 0), self.right, self.sent, self.got)
        self.first_l.wait_recv()
        added = self.at(3)[1][...].astype(f32) + self.held(0, 1)[...].astype(f32)
        self.held(2, 1)[...] = added.astype(bf16)
        self.comm.send(self.held(2, 1), self.held(3, 1), self.left, self.sent, self.got)

    def total(self):
        wait_all(self.got, self.two_blocks)
        return [
            own[...].astype(f32)
            + self.held(3, i)[...].astype(f32)
            + self.held(1, i)[...].astype(f32)
            for i, own in enumerate(self.at(0))
        ]


def z_offsets():
    return list(range(1, NZ))


def zc_offsets():
    return [(kz, kc) for kz in range(NZ) for kc in range(NC) if (kz, kc) != (0, 0)]


def unit_rows(values):
    floats = values.astype(f32)
    inverse = lax.rsqrt(jnp.sum(floats * floats, axis=1, keepdims=True) + 1e-06)
    return (floats * inverse, inverse)


def unit_back(normed, inverse, grad):
    return inverse * (grad - normed * jnp.sum(grad * normed, axis=1, keepdims=True))


def layer_norm(values):
    center = values - jnp.mean(values, axis=1, keepdims=True)
    scale_inv = lax.rsqrt(jnp.mean(center * center, axis=1, keepdims=True) + 1e-05)
    return (center * scale_inv, scale_inv)


def norm_back(grad, normed, scale_inv):
    return scale_inv * (
        grad
        - jnp.mean(grad, axis=1, keepdims=True)
        - normed * jnp.mean(grad * normed, axis=1, keepdims=True)
    )


def contract_last(left, right):
    return lax.dot_general(left, right, (((1,), (1,)), ((), ())), preferred_element_type=f32)


def contract_first(left, right):
    return lax.dot_general(left, right, (((0,), (0,)), ((), ())), preferred_element_type=f32)


def dot(left, right):
    return jnp.dot(left, right, preferred_element_type=f32)


def at(index, size):
    return pl.ds(pl.multiple_of(index * size, size), size)


def chunks(total, size):
    return [(i, min(size, total - i)) for i in range(0, total, size)]


def to_column(row, n):
    return jnp.transpose(jnp.broadcast_to(row, (128, n)))[:, 0:1]


def to_row(column, n):
    return jnp.transpose(jnp.broadcast_to(column, (n, 128)))[0:1]


def merged_lse(parts, count):
    peak = parts[0, 0:1]
    for i in range(1, count):
        peak = jnp.maximum(peak, parts[i, 0:1])
    total = jnp.zeros_like(peak)
    for i in range(count):
        total = total + parts[i, 1:2] * jnp.exp(parts[i, 0:1] - peak)
    return peak + jnp.log(total)


def body(
    img_hbm, txt_hbm, lab_hbm, lin_hbm, g1_hbm, g2_hbm, up_hbm, down_hbm, proj_hbm,
    text_hbm, input_hbm, up_grad_hbm, proj_grad_hbm,
    img_ref, txt_ref, lab_ref, lin_ref, g1_ref, g2_ref, text_out, input_out, up_out, proj_out, up_f, proj_f,
    w_up, w_down, w_proj, img_all, txt_all, lab_all, mlp_t, pooled_t, act, slope,
    res_out, res_in, n_in, n_out, logits, row_st, col_st, col_lse, rows_all, cols_all,
    grad, pimg, r_held, img_sum, img_mate, ptxt, sib_in, txo, t_held, tyo, tyi, tsum,
    rgrad, cot, cot_two, pre_out, pre_all, mg_out, mg_in,
    wpo, wpi, wp_sum, wpy, wpyi, wpz, wpzi, wpl, wu, wui, wyo, wyi, wsum, wblk,
    sems, ls,
):
    x, yl, z, c, t = coords()
    me = lax.axis_index("dp")
    rows, embed = img_ref.shape
    width = lin_ref.shape[1]
    half = rows // 2
    hidden = up_hbm.shape[1]
    hid = hidden // 8
    eh = embed // 2
    sib, mate, ynb = (dp_of(x, yl, z, 1 - c), t), (me, 1 - t), (dp_of(x, 1 - yl, z, c), t)
    zp = [(dp_of(x, yl, (z + k) % NZ, c), t) for k in range(1, NZ)]
    xp = [(dp_of((x + k) % NX, yl, z, c), t) for k in range(1, NX)]
    zc = [(dp_of(x, yl, (z + kz) % NZ, (c + kc) % NC), t) for kz, kc in zc_offsets()]
    row_peers = [
        (dp_of(x, yl, (z + k) % NZ, c), (t + j) % 2) for k in range(NZ) for j in range(2) if k or j
    ]
    col_peers = [
        (dp_of((x + kx) % NX, (yl + ky) % NYL, z, (c + kc) % NC), t)
        for kx in range(NX)
        for ky in range(NYL)
        for kc in range(NC)
        if kx or ky or kc
    ]
    cross = [p for (kz, kc), p in zip(zc_offsets(), zc) if kz and kc]
    greet = row_peers + col_peers + cross
    entry = pltpu.get_barrier_semaphore()
    small = [
        pltpu.make_async_copy(src, dst, ls.at[i])
        for i, (src, dst) in enumerate(
            [
                (img_hbm, img_ref),
                (txt_hbm, txt_ref),
                (lab_hbm, lab_ref),
                (lin_hbm, lin_ref),
                (g1_hbm, g1_ref),
                (g2_hbm, g2_ref),
            ]
        )
    ]
    loads = [
        pltpu.make_async_copy(up_hbm, w_up, ls.at[6]),
        pltpu.make_async_copy(down_hbm, w_down, ls.at[7]),
        pltpu.make_async_copy(proj_hbm, w_proj, ls.at[8]),
    ]
    for copy in small + loads:
        copy.start()
    for peer in greet:
        pl.semaphore_signal(entry, inc=1, device_id=peer, device_id_type=MESH)
    for copy in small:
        copy.wait()
    gain1, gain2 = g1_ref[...][None, :], g2_ref[...][None, :]
    my_slot = c * 8 + x * NYL + yl
    img_unit, _ = unit_rows(img_ref[...])
    img_all[at(z, rows)] = img_unit.astype(bf16)
    txt_unit, _ = unit_rows(txt_ref[at(t, half)])
    txt_all[at(my_slot, half)] = txt_unit.astype(bf16)
    lab_all[z] = jnp.broadcast_to(lab_ref[...][None, :], (8, rows))
    pl.semaphore_wait(entry, len(greet))

    comm = Comm(sems)
    send, new = comm.send, comm.new

    def same(ref, index, size, dev, sent=None, got=None):
        return send(ref.at[at(index, size)], ref.at[at(index, size)], dev, sent, got)

    txt_sent, img_sent, lab_sent, sib_got, lab_got = [new() for _ in range(5)]
    t_y = same(txt_all, my_slot, half, ynb, txt_sent)

    def txt_slot(part):
        return lambda pos: c * 8 + pos * NYL + part

    t_x = Ring(comm, txt_all, half, txt_slot(yl), x, xp, txt_sent)
    i_z = Ring(comm, img_all, rows, lambda pos: pos, z, zp, img_sent)
    for p in zp:
        send(lab_all.at[z], lab_all.at[z], p, lab_sent, lab_got)
    same(txt_all, my_slot, half, sib, txt_sent, sib_got)

    inputs = lin_ref[...].astype(f32)
    normed_in, inv_in = layer_norm(inputs)
    n_in[...] = normed_in
    mlp_in = (n_in[...] * gain1).astype(bf16)
    my_zc = z * NC + c
    for i, n in chunks(width, 128):
        mlp_t[i : i + n, at(my_zc, 128)] = jnp.transpose(
            n_in[:, i : i + n] * gain1[:, i : i + n]
        ).astype(bf16)
    loads[0].wait()

    def up_tile(i, _):
        cols = at(i, 512)
        pre = dot(mlp_in, w_up[:, cols])
        phi = 0.5 * (1.0 + lax.erf(pre * 0.7071067811865476))
        act[:, cols] = (pre * phi).astype(bf16)
        slope[:, cols] = phi + pre * jnp.exp(-0.5 * pre * pre) * 0.3989422804014327
        return _

    lax.fori_loop(0, hidden // 512, up_tile, 0)
    def to_sibling(part, offsets):
        for k in offsets:
            same(txt_all, txt_slot(part)((x + k) % NX), half, sib, txt_sent, sib_got)

    t_x.forward()
    t_y.wait_recv()
    f_x = Ring(comm, txt_all, half, txt_slot(1 - yl), x, xp, txt_sent)
    to_sibling(1 - yl, [0])
    i_z.forward()
    loads[1].wait()
    acts = act[...]
    for i, n in chunks(width, width // 2):
        if i:
            f_x.forward()
        res_out[:, i : i + n] = contract_last(acts, w_down[i : i + n]).astype(bf16)
    res_c = send(res_out, res_in, mate)
    t_x.near()
    to_sibling(yl, [1, 3])
    t_x.far()
    to_sibling(yl, [2])
    f_x.near()
    to_sibling(1 - yl, [1, 3])
    i_z.near()
    f_x.far()
    to_sibling(1 - yl, [2])
    i_z.far()
    mlp_sent, mlp_got, mlp_z = new(), new(), []

    def share_mlp(first, size):
        ref = mlp_t.at[first : first + size, at(my_zc, 128)]
        mlp_z.append((first, size, new()))
        for p in zp:
            send(ref, ref, p, mlp_sent, mlp_z[-1][2])
        send(ref, ref, sib, mlp_sent, mlp_got)

    def pass_mlp():
        for first, size, got in mlp_z:
            wait_all(got, mlp_t.at[first : first + size, 0:384])
            for k in range(1, NZ):
                ref = mlp_t.at[first : first + size, at(((z + k) % NZ) * NC + c, 128)]
                send(ref, ref, sib, mlp_sent, mlp_got)

    cut_a, cut_b = 512, 768
    share_mlp(0, cut_a)
    n_row, n_col = img_all.shape[0], txt_all.shape[0]
    tile = 256

    col_sent, col_got, row_sent, row_got = [new() for _ in range(4)]
    my_col = (x * NYL + yl) * NC + c
    wide = 2 * tile

    def side_totals(order):
        index = (c + order) % 2
        cols = at(index, wide)
        part = logit_scale * contract_last(img_all[...], txt_all[cols])
        logits[:, cols] = part
        col_peak = jnp.max(part, axis=0, keepdims=True)
        col_st[index, 0:1] = col_peak
        col_st[index, 1:2] = jnp.sum(jnp.exp(part - col_peak), axis=0, keepdims=True)
        for p in col_peers:
            send(col_st.at[index], cols_all.at[my_col, index], p, col_sent, col_got)
        peak = jnp.max(part, axis=1, keepdims=True)
        return peak, jnp.sum(jnp.exp(part - peak), axis=1, keepdims=True)

    peak_a, total_a = side_totals(0)
    wait_all(sib_got, txt_all.at[0 : 8 * half])
    wait_all(lab_got, lab_all.at[0:3])
    peak_b, total_b = side_totals(1)
    row_peak = jnp.maximum(peak_a, peak_b)
    row_total = total_a * jnp.exp(peak_a - row_peak) + total_b * jnp.exp(peak_b - row_peak)
    my_row = z * 2 + t
    row_st[0:1] = to_row(row_peak, n_row)
    row_st[1:2] = to_row(row_total, n_row)
    for p in row_peers:
        send(row_st, rows_all.at[my_row], p, row_sent, row_got)
    rows_all[my_row] = row_st[...]
    cols_all[my_col] = col_st[...]

    wait_all(col_got, cols_all.at[0:15])
    res_c.wait()
    resid = lin_ref[...].astype(f32) + (res_out[...].astype(f32) + res_in[...].astype(f32))
    normed_out, inv_out = layer_norm(resid)
    n_out[...] = normed_out
    for i, n in chunks(width, 128):
        pooled_t[i : i + n, at(c, rows)] = jnp.transpose(
            n_out[:, i : i + n] * gain2[:, i : i + n]
        ).astype(bf16)
    pool_s = send(
        pooled_t.at[:, at(c, rows)], pooled_t.at[:, at(c, rows)], sib
    )
    wait_all(row_got, rows_all.at[0:7])
    share_mlp(cut_a, cut_b - cut_a)

    row_lse = to_column(merged_lse(rows_all, 8), n_row)
    for i in range(2):
        col_lse[:, wide * i : wide * (i + 1)] = merged_lse(cols_all[:, i], 16)
    label_col = jnp.concatenate(
        [to_column(lab_all[i, 0:1].astype(f32), rows) for i in range(NZ)], axis=0
    )

    def grad_tile(i, _):
        cols = at(i, tile)
        part = logits[:, cols]
        place = i * tile + lax.broadcasted_iota(jnp.int32, (1, tile), 1)
        slot = place // half
        index = (((slot % (NX * NYL)) * NZ + z) * NC + slot // (NX * NYL)) * rows
        index = (index + t * half + place % half).astype(f32)
        value = 0.5 * (jnp.exp(part - row_lse) + jnp.exp(part - col_lse[:, cols]))
        value = value - jnp.where(label_col == index, 1.0, 0.0)
        grad[:, cols] = value.astype(bf16)
        return _

    lax.fori_loop(0, n_col // tile, grad_tile, 0)

    def strip(part, cols):
        return lambda pos: pimg.at[
            pl.ds(pl.multiple_of(pos * rows + part * half, half), half), cols
        ]

    def image_held(cols):
        return lambda kind, part: r_held.at[kind, part, :, cols]

    parts = [slice(0, 384), slice(384, 768), slice(768, 1024), slice(1024, embed)]
    ring_sent = new()
    sums = [
        RingSum(
            comm, strip(0, cols), strip(1, cols), image_held(cols), z, zp, ring_sent,
            pimg.at[0 : 2 * rows, cols],
        )
        for cols in parts
    ]
    for cols, ring in zip(parts, sums):
        pimg[:, cols] = (logit_scale * dot(grad[...], txt_all[:, cols])).astype(bf16)
        ring.first()
    for cols, ring in zip(parts, sums):
        ring.near()
        ptxt[:, cols] = (logit_scale * contract_first(grad[...], img_all[:, cols])).astype(bf16)
        ring.pass_on()
    share_mlp(cut_b, width - cut_b)

    side = 8 * half
    def text_sum():
        to_sib.wait()
        for pos in range(NX):
            mine = ptxt[pl.ds(pl.multiple_of(c * side + pos * pair, pair), pair)]
            txo[pos] = (
                mine.astype(f32) + sib_in[pos * pair : (pos + 1) * pair].astype(f32)
            ).astype(bf16)
        text_ring.first()
        text_ring.near()

    pair = 2 * half
    text_sent = new()
    text_ring = RingSum(
        comm,
        lambda pos: txo.at[pos, 0:half],
        lambda pos: txo.at[pos, half:],
        lambda kind, part: t_held.at[kind, part],
        x,
        xp,
        text_sent,
        txo.at[0:2],
    )
    mate_sent, mate_got = new(), new()

    def image_part(i):
        cols = parts[i]
        top, low = sums[i].total()
        img_sum[0:half, cols] = top.astype(bf16)
        img_sum[half:, cols] = low.astype(bf16)
        send(img_sum.at[:, cols], img_mate.at[:, cols], mate, mate_sent, mate_got)

    to_sib = send(ptxt.at[at(1 - c, side)], sib_in, sib)
    image_part(0)
    image_part(1)
    text_sum()
    image_part(2)
    image_part(3)
    loads[2].wait()
    wait_all(mate_got, img_mate)
    unit_grad = img_sum[...].astype(f32) + img_mate[...].astype(f32)
    img_norm, img_inv = unit_rows(img_ref[...])
    image_grad = unit_back(img_norm, img_inv, unit_grad)
    cotangent = image_grad.astype(bf16)
    cot[...] = cotangent
    cot_two[at(c, rows)] = cot[:, at(t, eh)]
    c_s = send(cot_two.at[at(c, rows)], cot_two.at[at(c, rows)], sib)
    eighth = width // 8
    rgrad[...] = contract_last(cotangent, w_proj[...]) * gain2
    p_cut = 112
    p_rows = (slice(0, p_cut), slice(p_cut, eighth))
    p_sent = new()
    p_ring = RingSum(
        comm,
        lambda pos: wpo.at[pos, p_rows[0]],
        lambda pos: wpo.at[pos, p_rows[1]],
        lambda kind, part: wpi.at[kind, p_rows[part]],
        x,
        xp,
        p_sent,
        wpo.at[0:2],
    )
    text_ring.pass_on()
    rgrad[...] = norm_back(rgrad[...], n_out[...], inv_out)
    resid_cot = rgrad[...].astype(bf16)
    g_sent, g_got = new(), new()
    for k in (2, 1, 3, 0):
        if k == 3:
            pool_s.wait()
            c_s.wait()
            for pos in range(NX):
                first = pl.multiple_of((2 * pos + c) * eighth, eighth)
                wpo[pos] = dot(pooled_t[pl.ds(first, eighth)], cot_two[...]).astype(bf16)
            p_ring.first()
            p_ring.near()
        other_z = (z + k) % NZ
        cols = at(other_z, 2 * hid)
        pre_out[:, cols] = (dot(resid_cot, w_down[:, cols]) * slope[:, cols]).astype(bf16)
        for j in range(NC):
            core = (c + j) % NC
            block = at(other_z * NC + core, hid)
            if k or j:
                send(
                    pre_out.at[:, block],
                    pre_all.at[at(my_zc, rows)],
                    (dp_of(x, yl, other_z, core), t),
                    g_sent,
                    g_got,
                )
            else:
                pre_all[at(my_zc, rows)] = pre_out[:, block]
    pass_mlp()
    pre_grad = pre_out[...]
    mg_sent, mg_got = new(), new()
    for i, n in chunks(width, 896):
        cols = slice(i, i + n)
        mg_out[:, cols] = contract_last(pre_grad, w_up[cols]).astype(bf16)
        send(mg_out.at[:, cols], mg_in.at[:, cols], mate, mg_sent, mg_got)
        if i == 0:
            tsum[0], tsum[1] = text_ring.total()
            tyo[...] = tsum[1 - yl].astype(bf16)
            y_t = send(tyo, tyi, ynb)
    p_ring.pass_on()

    wait_all(mlp_got, mlp_t.at[:, 0:512])
    wait_all(g_got, pre_all.at[0 : 7 * rows])

    wu_sent = new()

    def wu_ring(part, q):
        return RingSum(
            comm,
            lambda pos: wu.at[pos * NYL + part, :, 0:128],
            lambda pos: wu.at[pos * NYL + part, :, 128:],
            lambda kind, side: wui.at[q, kind, :, 128 * side : 128 * (side + 1)],
            x,
            xp,
            wu_sent,
            wu.at[0:2],
        )

    def wu_block(offset):
        pos = (x + offset) % NX
        wide = dot(mlp_t[at(pos, 2 * eighth)], pre_all[...]).astype(bf16)
        wu[NYL * pos], wu[NYL * pos + 1] = wide[0:eighth], wide[eighth:]

    ring_a, ring_b = wu_ring(1 - yl, 0), wu_ring(yl, 1)
    wu_block(2)
    ring_a.first()
    wu_block(1)
    wu_block(3)
    ring_a.near()
    ring_b.first()
    wu_block(0)
    for i, total in enumerate(p_ring.total()):
        wp_sum[p_rows[i]] = total
    share = eighth // 8
    for i in range(NZ):
        wpz[i, 0 : 2 * share] = wp_sum[2 * share * i : 2 * share * (i + 1)].astype(bf16)
        wpz[i, 2 * share :] = jnp.zeros((64 - 2 * share, eh), bf16)
    pz_sent, pz_got = new(), new()
    for k, p in zip(range(1, NZ), zp):
        send(wpz.at[(z + k) % NZ], wpzi.at[k - 1], p, pz_sent, pz_got)
    p_y = comm.make(wpy, wpyi, ynb)
    p_l = comm.make(wpl.at[1 - c], proj_out, sib)

    ring_a.pass_on()
    ring_b.near()
    y_t.wait()
    txt_norm, txt_inv = unit_rows(txt_ref[at(t, half)])
    text_out[at(t, half)] = unit_back(
        txt_norm, txt_inv, tsum[yl] + tyi[...].astype(f32)
    ).astype(bf16)
    t_m = same(text_out, t, half, mate)
    ring_b.pass_on()

    top, low = ring_a.total()
    wyo[:, 0:128] = top.astype(bf16)
    wyo[:, 128:] = low.astype(bf16)
    w_y = send(wyo, wyi, ynb)
    wait_all(mg_got, mg_in)
    dm = (mg_out[...].astype(f32) + mg_in[...].astype(f32)) * gain1
    input_out[...] = (rgrad[...] + norm_back(dm, n_in[...], inv_in)).astype(bf16)
    stores = [
        pltpu.make_async_copy(src, dst, ls.at[9 + i])
        for i, (src, dst) in enumerate(
            [
                (input_out, input_hbm),
                (text_out, text_hbm),
                (up_f, up_grad_hbm),
                (proj_f, proj_grad_hbm),
            ]
        )
    ]
    stores[0].start()

    wait_all(pz_got, wpzi)
    total = wpz[z].astype(f32)
    for k in range(NZ - 1):
        total = total + wpzi[k].astype(f32)
    wp_sum[0:64] = total
    wpy[...] = total.astype(bf16)

    @pl.when(c != yl)
    def _():
        p_y.start()

    top, low = ring_b.total()
    wsum[:, 0:128] = top
    wsum[:, 128:] = low
    w_y.wait()
    wsum[...] = wsum[...] + wyi[...].astype(f32)
    for i in range(8):
        wblk[i, 0:share] = wsum[share * i : share * (i + 1)].astype(bf16)
        wblk[i, share:] = jnp.zeros((32 - share, hid), bf16)
    last_sent, last_got = new(), new()
    for (kz, kc), p in zip(zc_offsets(), zc):
        slot = ((z + kz) % NZ) * NC + (c + kc) % NC
        send(wblk.at[slot], up_out.at[:, at(my_zc, hid)], p, last_sent, last_got)
    up_out[:, at(my_zc, hid)] = wblk[my_zc]

    @pl.when(c == yl)
    def _():
        p_y.wait_recv()
        wp_sum[0:64] = wp_sum[0:64] + wpyi[...].astype(f32)
        for i in range(NC):
            wpl[i, 0:share] = wp_sum[share * i : share * (i + 1)]
            wpl[i, share:] = jnp.zeros((32 - share, eh), f32)
        p_l.start()
        proj_out[...] = wpl[c]
        p_l.wait_send()

    @pl.when(c != yl)
    def _():
        p_y.wait_send()
        p_l.wait_recv()

    proj_f[...] = proj_out[0:share]
    stores[3].start()
    t_m.wait()
    stores[1].start()
    wait_all(last_got, up_out.at[:, 0 : 7 * hid])
    up_f[...] = up_out[0:share].astype(f32)
    stores[2].start()
    for sem, ref in (
        (txt_sent, txt_all.at[0 : 15 * half]),
        (img_sent, img_all.at[0 : 3 * rows]),
        (lab_sent, lab_all.at[0:3]),
        (mlp_sent, mlp_t.at[:, 0 : 7 * 128]),
        (col_sent, cols_all.at[0:15]),
        (row_sent, rows_all.at[0:7]),
        (ring_sent, pimg.at[0 : 3 * rows]),
        (mate_sent, img_mate),
        (text_sent, txo.at[0:3]),
        (p_sent, wpo.at[0:3]),
        (g_sent, pre_all.at[0 : 7 * rows]),
        (mg_sent, mg_in),
        (wu_sent, wu.at[0:6]),
        (pz_sent, wpzi),
        (last_sent, up_out.at[:, 0 : 7 * hid]),
    ):
        wait_all(sem, ref)
    for copy in stores:
        copy.wait()


def finish(*refs):
    for src, dst in zip(refs[:4], refs[4:]):
        dst[...] = src[...]


def local(image_cache, text_cache, labels, layer_input, ln1_gain, ln2_gain, w_up, w_down, proj):
    rows, embed = image_cache.shape
    width = layer_input.shape[1]
    half = rows // 2
    hidden = w_up.shape[1]
    hid = hidden // 8
    eh = embed // 2
    eighth = width // 8
    share = width // 64
    n_sems = 83
    vm = pltpu.VMEM
    scratch = [
        vm((rows, embed), bf16),
        vm((rows, embed), bf16),
        vm((rows,), jnp.int32),
        vm((rows, width), bf16),
        vm((width,), f32),
        vm((width,), f32),
        vm((rows, embed), bf16),
        vm((rows, width), bf16),
        vm((32, hidden), bf16),
        vm((32, eh), f32),
        vm((width // 64, hidden), f32),
        vm((width // 64, eh), f32),
        vm(w_up.shape, bf16),
        vm(w_down.shape, bf16),
        vm(proj.shape, bf16),
        vm((NZ * rows, embed), bf16),
        vm((16 * half, embed), bf16),
        vm((NZ, 8, rows), jnp.int32),
        vm((width, 8 * rows), bf16),
        vm((width, 2 * rows), bf16),
        vm((rows, hidden), bf16),
        vm((rows, hidden), f32),
        vm((rows, width), bf16),
        vm((rows, width), bf16),
        vm((rows, width), f32),
        vm((rows, width), f32),
        vm((NZ * rows, 16 * half), f32),
        vm((2, NZ * rows), f32),
        vm((2, 2, 8 * half), f32),
        vm((1, 16 * half), f32),
        vm((8, 2, NZ * rows), f32),
        vm((16, 2, 2, 8 * half), f32),
        vm((NZ * rows, 16 * half), bf16),
        vm((NZ * rows, embed), bf16),
        vm((4, 2, half, embed), bf16),
        vm((rows, embed), bf16),
        vm((rows, embed), bf16),
        vm((16 * half, embed), bf16),
        vm((8 * half, embed), bf16),
        vm((NX, 2 * half, embed), bf16),
        vm((4, 2, half, embed), bf16),
        vm((half, embed), bf16),
        vm((half, embed), bf16),
        vm((2, half, embed), f32),
        vm((rows, width), f32),
        vm((rows, embed), bf16),
        vm((2 * rows, eh), bf16),
        vm((rows, hidden), bf16),
        vm((8 * rows, hid), bf16),
        vm((rows, width), bf16),
        vm((rows, width), bf16),
        vm((NX, eighth, eh), bf16),
        vm((4, eighth, eh), bf16),
        vm((eighth, eh), f32),
        vm((64, eh), bf16),
        vm((64, eh), bf16),
        vm((NZ, 64, eh), bf16),
        vm((NZ - 1, 64, eh), bf16),
        vm((NC, 32, eh), f32),
        vm((8, eighth, hid), bf16),
        vm((2, 4, eighth, hid), bf16),
        vm((eighth, hid), bf16),
        vm((eighth, hid), bf16),
        vm((eighth, hid), f32),
        vm((8, 32, hid), bf16),
        pltpu.SemaphoreType.DMA((n_sems,)),
        pltpu.SemaphoreType.DMA((13,)),
    ]
    anywhere = pl.BlockSpec(memory_space=pl.ANY)
    on_vmem = pl.BlockSpec(memory_space=pltpu.VMEM)
    parts = pl.pallas_call(
        body,
        name="clip_mlp",
        out_shape=[
            jax.ShapeDtypeStruct((rows, embed), bf16),
            jax.ShapeDtypeStruct((rows, width), bf16),
            jax.ShapeDtypeStruct((width // 64, hidden), f32),
            jax.ShapeDtypeStruct((width // 64, eh), f32),
        ],
        in_specs=[anywhere] * 9,
        out_specs=[anywhere] * 4,
        scratch_shapes=scratch,
        compiler_params=pltpu.CompilerParams(
            collective_id=1, has_side_effects=True, vmem_limit_bytes=VMEM_LIMIT
        ),
    )(
        image_cache,
        text_cache,
        labels,
        layer_input,
        ln1_gain,
        ln2_gain,
        w_up,
        w_down,
        proj,
    )
    return pl.pallas_call(
        finish,
        name="finish",
        out_shape=[
            jax.ShapeDtypeStruct((rows, embed), bf16),
            jax.ShapeDtypeStruct((rows, width), bf16),
            jax.ShapeDtypeStruct((share, hidden), f32),
            jax.ShapeDtypeStruct((share, eh), f32),
        ],
        in_specs=[on_vmem] * 4,
        out_specs=[on_vmem] * 4,
    )(*parts)


def solution(mesh):
    in_specs = (
        P("dp", None),
        P("dp", None),
        P("dp"),
        P("dp", None),
        P(),
        P(),
        P(None, "tensor"),
        P(None, "tensor"),
        P(),
    )
    out_specs = (P("dp", None), P("dp", None), P("dp", "tensor"), P("dp", "tensor"))
    return jax.shard_map(local, mesh=mesh, in_specs=in_specs, out_specs=out_specs, check_vma=False)
```

time: 97.8 us -> 91.1 us (0.931)
  the two profiles are of different devices: /device:TPU:17 before, /device:TPU:1 now
where the time goes in v5:
time: 91.1 us; the launch traced here: 91 us
  Pallas kernels  90.3 us (99%)
    pallas_call x1, Pallas kernels, local(): pl.pallas_call(body, name='clip_mlp', out_shape=[jax.ShapeDtypeStruct((ro...  88.1 us
    pallas_call x1, Pallas kernels, local(): pl.pallas_call(finish, name='finish', out_shape=[jax.ShapeDtypeStruct((ro...  2.2 us

profile of v5, /device:TPU:1, one launch (start us, length us, event | category | flops | bytes accessed | tf_op | source)
XLA Modules:
  0.0 91.0 jit_solution(6965861052114753820)
XLA Ops:
  0.6 88.1 %clip_mlp.1 = (bf16[128,1280]{1,0:T(8,128)(2,1)}, bf16[128,1664]{1,0:T(8,128)(2,1)}, f32[26,2048]{1,0:T(8,128)}, f32[26,640]{1,0:T(8,128)}) custom-call(bf16[128,1280]{1,0:T(8,128)(2,1)} %img_hbm.1, bf16[128,1280]{1,0:T(8,128)(2,1)} %txt_hbm.1, s32[128]{0:T(128)} %lab_hbm.1, bf16[128,1664]{1,0:T(8,128)(2,1)} %lin_hbm.1, f32[1664]{0:T(1024)} %g1_hbm.1, ...), custom_call_target="tpu_custom_call" | custom-call | tf_op jit(solution)/shard_map/clip_mlp/pallas_call | solution.py:775
  88.8 2.2 %finish.1 = (bf16[128,1280]{1,0:T(8,128)(2,1)}, bf16[128,1664]{1,0:T(8,128)(2,1)}, f32[26,2048]{1,0:T(8,128)}, f32[26,640]{1,0:T(8,128)}) custom-call(bf16[128,1280]{1,0:T(8,128)(2,1)} %get-tuple-element.8.refs_0_, bf16[128,1664]{1,0:T(8,128)(2,1)} %get-tuple-element.9.refs_1_, f32[26,2048]{1,0:T(8,128)} %get-tuple-element.10.refs_2_, ...), custom_call_target="tpu_custom_call" | custom-call | tf_op jit(solution)/shard_map/finish/pallas_call | solution.py:801

commit v6 on v5

--- a/solution.py
+++ b/solution.py
@@ -341,7 +341,7 @@
                 ref = mlp_t.at[first : first + size, at(((z + k) % NZ) * NC + c, 128)]
                 send(ref, ref, sib, mlp_sent, mlp_got)
 
-    cut_a, cut_b = 512, 768
+    cut_a, cut_b = 512, 1152
     share_mlp(0, cut_a)
     n_row, n_col = img_all.shape[0], txt_all.shape[0]
     tile = 256
@@ -374,6 +374,7 @@
     row_st[1:2] = to_row(row_total, n_row)
     for p in row_peers:
         send(row_st, rows_all.at[my_row], p, row_sent, row_got)
+    share_mlp(cut_a, cut_b - cut_a)
     rows_all[my_row] = row_st[...]
     cols_all[my_col] = col_st[...]
 
@@ -390,7 +391,6 @@
         pooled_t.at[:, at(c, rows)], pooled_t.at[:, at(c, rows)], sib
     )
     wait_all(row_got, rows_all.at[0:7])
-    share_mlp(cut_a, cut_b - cut_a)
 
     row_lse = to_column(merged_lse(rows_all, 8), n_row)
     for i in range(2):
@@ -421,7 +421,7 @@
     def image_held(cols):
         return lambda kind, part: r_held.at[kind, part, :, cols]
 
-    parts = [slice(0, 384), slice(384, 768), slice(768, 1024), slice(1024, embed)]
+    parts = [slice(0, 384), slice(384, 768), slice(768, 1152), slice(1152, embed)]
     ring_sent = new()
     sums = [
         RingSum(
@@ -433,15 +433,16 @@
     for cols, ring in zip(parts, sums):
         pimg[:, cols] = (logit_scale * dot(grad[...], txt_all[:, cols])).astype(bf16)
         ring.first()
+    side = 8 * half
+    part_sent, part_got = new(), new()
     for cols, ring in zip(parts, sums):
         ring.near()
         ptxt[:, cols] = (logit_scale * contract_first(grad[...], img_all[:, cols])).astype(bf16)
+        send(ptxt.at[at(1 - c, side), cols], sib_in.at[:, cols], sib, part_sent, part_got)
         ring.pass_on()
-    share_mlp(cut_b, width - cut_b)
-
-    side = 8 * half
+
     def text_sum():
-        to_sib.wait()
+        wait_all(part_got, sib_in)
         for pos in range(NX):
             mine = ptxt[pl.ds(pl.multiple_of(c * side + pos * pair, pair), pair)]
             txo[pos] = (
@@ -471,13 +472,14 @@
         img_sum[half:, cols] = low.astype(bf16)
         send(img_sum.at[:, cols], img_mate.at[:, cols], mate, mate_sent, mate_got)
 
-    to_sib = send(ptxt.at[at(1 - c, side)], sib_in, sib)
     image_part(0)
+    text_sum()
     image_part(1)
-    text_sum()
     image_part(2)
     image_part(3)
+    share_mlp(cut_b, width - cut_b)
     loads[2].wait()
+    text_ring.pass_on()
     wait_all(mate_got, img_mate)
     unit_grad = img_sum[...].astype(f32) + img_mate[...].astype(f32)
     img_norm, img_inv = unit_rows(img_ref[...])
@@ -501,7 +503,6 @@
         p_sent,
         wpo.at[0:2],
     )
-    text_ring.pass_on()
     rgrad[...] = norm_back(rgrad[...], n_out[...], inv_out)
     resid_cot = rgrad[...].astype(bf16)
     g_sent, g_got = new(), new()
@@ -530,6 +531,9 @@
                 )
             else:
                 pre_all[at(my_zc, rows)] = pre_out[:, block]
+    tsum[0], tsum[1] = text_ring.total()
+    tyo[...] = tsum[1 - yl].astype(bf16)
+    y_t = send(tyo, tyi, ynb)
     pass_mlp()
     pre_grad = pre_out[...]
     mg_sent, mg_got = new(), new()
@@ -537,11 +541,13 @@
         cols = slice(i, i + n)
         mg_out[:, cols] = contract_last(pre_grad, w_up[cols]).astype(bf16)
         send(mg_out.at[:, cols], mg_in.at[:, cols], mate, mg_sent, mg_got)
-        if i == 0:
-            tsum[0], tsum[1] = text_ring.total()
-            tyo[...] = tsum[1 - yl].astype(bf16)
-            y_t = send(tyo, tyi, ynb)
     p_ring.pass_on()
+
+    y_t.wait()
+    txt_norm, txt_inv = unit_rows(txt_ref[at(t, half)])
+    text_out[at(t, half)] = unit_back(
+        txt_norm, txt_inv, tsum[yl] + tyi[...].astype(f32)
+    ).astype(bf16)
 
     wait_all(mlp_got, mlp_t.at[:, 0:512])
     wait_all(g_got, pre_all.at[0 : 7 * rows])
@@ -573,6 +579,8 @@
     ring_a.near()
     ring_b.first()
     wu_block(0)
+    ring_a.pass_on()
+    ring_b.near()
     for i, total in enumerate(p_ring.total()):
         wp_sum[p_rows[i]] = total
     share = eighth // 8
@@ -585,20 +593,13 @@
     p_y = comm.make(wpy, wpyi, ynb)
     p_l = comm.make(wpl.at[1 - c], proj_out, sib)
 
-    ring_a.pass_on()
-    ring_b.near()
-    y_t.wait()
-    txt_norm, txt_inv = unit_rows(txt_ref[at(t, half)])
-    text_out[at(t, half)] = unit_back(
-        txt_norm, txt_inv, tsum[yl] + tyi[...].astype(f32)
-    ).astype(bf16)
-    t_m = same(text_out, t, half, mate)
     ring_b.pass_on()
 
     top, low = ring_a.total()
     wyo[:, 0:128] = top.astype(bf16)
     wyo[:, 128:] = low.astype(bf16)
     w_y = send(wyo, wyi, ynb)
+    t_m = same(text_out, t, half, mate)
     wait_all(mg_got, mg_in)
     dm = (mg_out[...].astype(f32) + mg_in[...].astype(f32)) * gain1
     input_out[...] = (rgrad[...] + norm_back(dm, n_in[...], inv_in)).astype(bf16)
@@ -672,6 +673,7 @@
         (row_sent, rows_all.at[0:7]),
         (ring_sent, pimg.at[0 : 3 * rows]),
         (mate_sent, img_mate),
+        (part_sent, sib_in),
         (text_sent, txo.at[0:3]),
         (p_sent, wpo.at[0:3]),
         (g_sent, pre_all.at[0 : 7 * rows]),

time: 91.1 us -> 84.4 us (0.926)
  Pallas kernels: 90.3 us -> 83.7 us
    pallas_call x1, Pallas kernels: 88.1 us -> 81.5 us  [local(): pl.pallas_call(body, name='clip_mlp', out_shape=[jax.ShapeDtypeStruct((ro...]
where the time goes in v6:
time: 84.4 us; the launch traced here: 84.3 us
  Pallas kernels  83.7 us (99%)
    pallas_call x1, Pallas kernels, local(): pl.pallas_call(body, name='clip_mlp', out_shape=[jax.ShapeDtypeStruct((ro...  81.5 us
    pallas_call x1, Pallas kernels, local(): pl.pallas_call(finish, name='finish', out_shape=[jax.ShapeDtypeStruct((ro...  2.2 us

profile of v6, /device:TPU:1, one launch (start us, length us, event | category | flops | bytes accessed | tf_op | source)
XLA Modules:
  0.0 84.3 jit_solution(12334692696350099218)
XLA Ops:
  0.6 81.5 %clip_mlp.1 = (bf16[128,1280]{1,0:T(8,128)(2,1)}, bf16[128,1664]{1,0:T(8,128)(2,1)}, f32[26,2048]{1,0:T(8,128)}, f32[26,640]{1,0:T(8,128)}) custom-call(bf16[128,1280]{1,0:T(8,128)(2,1)} %img_hbm.1, bf16[128,1280]{1,0:T(8,128)(2,1)} %txt_hbm.1, s32[128]{0:T(128)} %lab_hbm.1, bf16[128,1664]{1,0:T(8,128)(2,1)} %lin_hbm.1, f32[1664]{0:T(1024)} %g1_hbm.1, ...), custom_call_target="tpu_custom_call" | custom-call | tf_op jit(solution)/shard_map/clip_mlp/pallas_call | solution.py:777
  82.1 2.2 %finish.1 = (bf16[128,1280]{1,0:T(8,128)(2,1)}, bf16[128,1664]{1,0:T(8,128)(2,1)}, f32[26,2048]{1,0:T(8,128)}, f32[26,640]{1,0:T(8,128)}) custom-call(bf16[128,1280]{1,0:T(8,128)(2,1)} %get-tuple-element.8.refs_0_, bf16[128,1664]{1,0:T(8,128)(2,1)} %get-tuple-element.9.refs_1_, f32[26,2048]{1,0:T(8,128)} %get-tuple-element.10.refs_2_, ...), custom_call_target="tpu_custom_call" | custom-call | tf_op jit(solution)/shard_map/finish/pallas_call | solution.py:803

commit v7 on v6

--- a/solution.py
+++ b/solution.py
@@ -196,7 +196,7 @@
     img_hbm, txt_hbm, lab_hbm, lin_hbm, g1_hbm, g2_hbm, up_hbm, down_hbm, proj_hbm,
     text_hbm, input_hbm, up_grad_hbm, proj_grad_hbm,
     img_ref, txt_ref, lab_ref, lin_ref, g1_ref, g2_ref, text_out, input_out, up_out, proj_out, up_f, proj_f,
-    w_up, w_down, w_proj, img_all, txt_all, lab_all, mlp_t, pooled_t, act, slope,
+    w_up, w_down, w_proj_t, img_all, txt_all, lab_all, mlp_t, pooled_t, act, slope,
     res_out, res_in, n_in, n_out, logits, row_st, col_st, col_lse, rows_all, cols_all,
     grad, pimg, r_held, img_sum, img_mate, ptxt, sib_in, txo, t_held, tyo, tyi, tsum,
     rgrad, cot, cot_two, pre_out, pre_all, mg_out, mg_in,
@@ -244,8 +244,11 @@
     loads = [
         pltpu.make_async_copy(up_hbm, w_up, ls.at[6]),
         pltpu.make_async_copy(down_hbm, w_down, ls.at[7]),
-        pltpu.make_async_copy(proj_hbm, w_proj, ls.at[8]),
     ]
+    homes = [(0, ptxt), (ptxt.shape[0], pimg), (ptxt.shape[0] + pimg.shape[0], img_sum)]
+    for i, (first, home) in enumerate(homes):
+        block = proj_hbm.at[first : first + home.shape[0]]
+        loads.append(pltpu.make_async_copy(block, home, ls.at[(8, 13, 14)[i]]))
     for copy in small + loads:
         copy.start()
     for peer in greet:
@@ -311,10 +314,9 @@
     loads[1].wait()
     acts = act[...]
     for i, n in chunks(width, width // 2):
-        if i:
-            f_x.forward()
         res_out[:, i : i + n] = contract_last(acts, w_down[i : i + n]).astype(bf16)
     res_c = send(res_out, res_in, mate)
+    f_x.forward()
     t_x.near()
     to_sibling(yl, [1, 3])
     t_x.far()
@@ -341,13 +343,13 @@
                 ref = mlp_t.at[first : first + size, at(((z + k) % NZ) * NC + c, 128)]
                 send(ref, ref, sib, mlp_sent, mlp_got)
 
-    cut_a, cut_b = 512, 1152
+    cut_a, cut_b = 512, 960
     share_mlp(0, cut_a)
     n_row, n_col = img_all.shape[0], txt_all.shape[0]
     tile = 256
 
     col_sent, col_got, row_sent, row_got = [new() for _ in range(4)]
-    my_col = (x * NYL + yl) * NC + c
+    my_col, my_row = (x * NYL + yl) * NC + c, z * 2 + t
     wide = 2 * tile
 
     def side_totals(order):
@@ -355,29 +357,43 @@
         cols = at(index, wide)
         part = logit_scale * contract_last(img_all[...], txt_all[cols])
         logits[:, cols] = part
+        peak = jnp.max(part, axis=1, keepdims=True)
+        total = jnp.sum(jnp.exp(part - peak), axis=1, keepdims=True)
+        if order:
+            row_peak = jnp.maximum(peak_a, peak)
+            row_st[0:1] = to_row(row_peak, n_row)
+            row_st[1:2] = to_row(
+                total_a * jnp.exp(peak_a - row_peak) + total * jnp.exp(peak - row_peak), n_row
+            )
+            for p in row_peers:
+                send(row_st, rows_all.at[my_row], p, row_sent, row_got)
         col_peak = jnp.max(part, axis=0, keepdims=True)
         col_st[index, 0:1] = col_peak
         col_st[index, 1:2] = jnp.sum(jnp.exp(part - col_peak), axis=0, keepdims=True)
         for p in col_peers:
             send(col_st.at[index], cols_all.at[my_col, index], p, col_sent, col_got)
-        peak = jnp.max(part, axis=1, keepdims=True)
-        return peak, jnp.sum(jnp.exp(part - peak), axis=1, keepdims=True)
+        return peak, total
 
     peak_a, total_a = side_totals(0)
     wait_all(sib_got, txt_all.at[0 : 8 * half])
     wait_all(lab_got, lab_all.at[0:3])
-    peak_b, total_b = side_totals(1)
-    row_peak = jnp.maximum(peak_a, peak_b)
-    row_total = total_a * jnp.exp(peak_a - row_peak) + total_b * jnp.exp(peak_b - row_peak)
-    my_row = z * 2 + t
-    row_st[0:1] = to_row(row_peak, n_row)
-    row_st[1:2] = to_row(row_total, n_row)
-    for p in row_peers:
-        send(row_st, rows_all.at[my_row], p, row_sent, row_got)
+    side_totals(1)
     share_mlp(cut_a, cut_b - cut_a)
     rows_all[my_row] = row_st[...]
     cols_all[my_col] = col_st[...]
 
+    for copy in loads[2:]:
+        copy.wait()
+    for first, home in homes:
+
+        def turn_tile(i, _):
+            w_proj_t[:, at(first // 128 + i, 128)] = jnp.transpose(home[at(i, 128)])
+            return _
+
+        lax.fori_loop(0, home.shape[0] // 128, turn_tile, 0)
+    label_col = jnp.concatenate(
+        [to_column(lab_all[i, 0:1].astype(f32), rows) for i in range(NZ)], axis=0
+    )
     wait_all(col_got, cols_all.at[0:15])
     res_c.wait()
     resid = lin_ref[...].astype(f32) + (res_out[...].astype(f32) + res_in[...].astype(f32))
@@ -395,9 +411,6 @@
     row_lse = to_column(merged_lse(rows_all, 8), n_row)
     for i in range(2):
         col_lse[:, wide * i : wide * (i + 1)] = merged_lse(cols_all[:, i], 16)
-    label_col = jnp.concatenate(
-        [to_column(lab_all[i, 0:1].astype(f32), rows) for i in range(NZ)], axis=0
-    )
 
     def grad_tile(i, _):
         cols = at(i, tile)
@@ -478,18 +491,17 @@
     image_part(2)
     image_part(3)
     share_mlp(cut_b, width - cut_b)
-    loads[2].wait()
     text_ring.pass_on()
+    img_norm, img_inv = unit_rows(img_ref[...])
     wait_all(mate_got, img_mate)
     unit_grad = img_sum[...].astype(f32) + img_mate[...].astype(f32)
-    img_norm, img_inv = unit_rows(img_ref[...])
     image_grad = unit_back(img_norm, img_inv, unit_grad)
     cotangent = image_grad.astype(bf16)
     cot[...] = cotangent
     cot_two[at(c, rows)] = cot[:, at(t, eh)]
     c_s = send(cot_two.at[at(c, rows)], cot_two.at[at(c, rows)], sib)
     eighth = width // 8
-    rgrad[...] = contract_last(cotangent, w_proj[...]) * gain2
+    rgrad[...] = dot(cotangent, w_proj_t[...]) * gain2
     p_cut = 112
     p_rows = (slice(0, p_cut), slice(p_cut, eighth))
     p_sent = new()
@@ -557,19 +569,18 @@
     def wu_ring(part, q):
         return RingSum(
             comm,
-            lambda pos: wu.at[pos * NYL + part, :, 0:128],
-            lambda pos: wu.at[pos * NYL + part, :, 128:],
+            lambda pos: wu.at[at(pos * NYL + part, eighth), 0:128],
+            lambda pos: wu.at[at(pos * NYL + part, eighth), 128:],
             lambda kind, side: wui.at[q, kind, :, 128 * side : 128 * (side + 1)],
             x,
             xp,
             wu_sent,
-            wu.at[0:2],
+            wu.at[0 : 2 * eighth],
         )
 
     def wu_block(offset):
-        pos = (x + offset) % NX
-        wide = dot(mlp_t[at(pos, 2 * eighth)], pre_all[...]).astype(bf16)
-        wu[NYL * pos], wu[NYL * pos + 1] = wide[0:eighth], wide[eighth:]
+        block = at((x + offset) % NX, 2 * eighth)
+        wu[block] = dot(mlp_t[block], pre_all[...]).astype(bf16)
 
     ring_a, ring_b = wu_ring(1 - yl, 0), wu_ring(yl, 1)
     wu_block(2)
@@ -678,7 +689,7 @@
         (p_sent, wpo.at[0:3]),
         (g_sent, pre_all.at[0 : 7 * rows]),
         (mg_sent, mg_in),
-        (wu_sent, wu.at[0:6]),
+        (wu_sent, wu.at[0 : 6 * eighth]),
         (pz_sent, wpzi),
         (last_sent, up_out.at[:, 0 : 7 * hid]),
     ):
@@ -718,7 +729,7 @@
         vm((width // 64, eh), f32),
         vm(w_up.shape, bf16),
         vm(w_down.shape, bf16),
-        vm(proj.shape, bf16),
+        vm((embed, width), bf16),
         vm((NZ * rows, embed), bf16),
         vm((16 * half, embed), bf16),
         vm((NZ, 8, rows), jnp.int32),
@@ -763,14 +774,14 @@
         vm((NZ, 64, eh), bf16),
         vm((NZ - 1, 64, eh), bf16),
         vm((NC, 32, eh), f32),
-        vm((8, eighth, hid), bf16),
+        vm((8 * eighth, hid), bf16),
         vm((2, 4, eighth, hid), bf16),
         vm((eighth, hid), bf16),
         vm((eighth, hid), bf16),
         vm((eighth, hid), f32),
         vm((8, 32, hid), bf16),
         pltpu.SemaphoreType.DMA((n_sems,)),
-        pltpu.SemaphoreType.DMA((13,)),
+        pltpu.SemaphoreType.DMA((15,)),
     ]
     anywhere = pl.BlockSpec(memory_space=pl.ANY)
     on_vmem = pl.BlockSpec(memory_space=pltpu.VMEM)

time: 84.4 us -> 83 us (0.983)
  Pallas kernels: 83.7 us -> 82.2 us
    pallas_call x1, Pallas kernels: 81.5 us -> 80 us  [local(): pl.pallas_call(body, name='clip_mlp', out_shape=[jax.ShapeDtypeStruct((ro...]
where the time goes in v7:
time: 83 us; the launch traced here: 82.8 us
  Pallas kernels  82.2 us (99%)
    pallas_call x1, Pallas kernels, local(): pl.pallas_call(body, name='clip_mlp', out_shape=[jax.ShapeDtypeStruct((ro...  80 us
    pallas_call x1, Pallas kernels, local(): pl.pallas_call(finish, name='finish', out_shape=[jax.ShapeDtypeStruct((ro...  2.2 us

profile of v7, /device:TPU:1, one launch (start us, length us, event | category | flops | bytes accessed | tf_op | source)
XLA Modules:
  0.0 82.8 jit_solution(6401741222450105007)
XLA Ops:
  0.6 80.0 %clip_mlp.1 = (bf16[128,1280]{1,0:T(8,128)(2,1)}, bf16[128,1664]{1,0:T(8,128)(2,1)}, f32[26,2048]{1,0:T(8,128)}, f32[26,640]{1,0:T(8,128)}) custom-call(bf16[128,1280]{1,0:T(8,128)(2,1)} %img_hbm.1, bf16[128,1280]{1,0:T(8,128)(2,1)} %txt_hbm.1, s32[128]{0:T(128)} %lab_hbm.1, bf16[128,1664]{1,0:T(8,128)(2,1)} %lin_hbm.1, f32[1664]{0:T(1024)} %g1_hbm.1, ...), custom_call_target="tpu_custom_call" | custom-call | tf_op jit(solution)/shard_map/clip_mlp/pallas_call | solution.py:788
  80.6 2.2 %finish.1 = (bf16[128,1280]{1,0:T(8,128)(2,1)}, bf16[128,1664]{1,0:T(8,128)(2,1)}, f32[26,2048]{1,0:T(8,128)}, f32[26,640]{1,0:T(8,128)}) custom-call(bf16[128,1280]{1,0:T(8,128)(2,1)} %get-tuple-element.8.refs_0_, bf16[128,1664]{1,0:T(8,128)(2,1)} %get-tuple-element.9.refs_1_, f32[26,2048]{1,0:T(8,128)} %get-tuple-element.10.refs_2_, ...), custom_call_target="tpu_custom_call" | custom-call | tf_op jit(solution)/shard_map/finish/pallas_call | solution.py:814
